TPU v7x, 256 devices: a whole 4x4x8 slice. The times are simulated.
256 devices in a mesh: inp: 8 (over z_lo, x), out: 4 (over y), dep: 8 (over z_hi, core).
Axes of the slice: x: 4, y: 4, z: 8 (z_hi: 4, z_lo: 2; z = z_hi * 2 + z_lo), core: 2. Of those that a mesh axis runs over, the one named last changes fastest.
Arguments:
- tokens: bfloat16 [1024, 4096], P(('dep', 'out'), 'inp'), may hold values from -6 to 6
- cotangent: bfloat16 [1024, 4096], P(('dep', 'out'), 'inp'), may hold values from -3 to 3
- gate_weight: bfloat16 [4096, 14336], P(('inp', 'dep'), 'out'), may hold values from -0.09375 to 0.09375
- up_weight: bfloat16 [4096, 14336], P(('inp', 'dep'), 'out'), may hold values from -0.09375 to 0.09375
- down_weight: bfloat16 [14336, 4096], P(('out', 'dep'), 'inp'), may hold values from -0.046875 to 0.046875
Outputs:
- token_grad: float32 [1024, 4096], P(('dep', 'out'), 'inp')
- gate_weight_grad: float32 [4096, 14336], P(('inp', 'dep'), 'out')
- up_weight_grad: float32 [4096, 14336], P(('inp', 'dep'), 'out')
- down_weight_grad: float32 [14336, 4096], P(('out', 'dep'), 'inp')
All inputs are finite; a program needn't handle non-finite values.
Results may differ from a plain program's by a relative error of at most 0.019.
Values may be sent and summed in bfloat16 or wider, within the bound.
A program may use at most 128 MiB of HBM per device.

v0:
```python
import jax
import jax.numpy as jnp
from jax import lax
from jax.sharding import PartitionSpec as P


def contract_last(left_side, right_side):
    return lax.dot_general(
        left_side, right_side, (((1,), (1,)), ((), ())), preferred_element_type=jnp.float32
    )


def contract_first(left_side, right_side):
    return lax.dot_general(
        left_side, right_side, (((0,), (0,)), ((), ())), preferred_element_type=jnp.float32
    )


def local_step(gate_value, up_value, hidden_grad):
    logistic = jax.nn.sigmoid(gate_value)
    activated = gate_value * logistic
    hidden = (activated * up_value).astype(jnp.bfloat16)
    up_grad = (hidden_grad * activated).astype(jnp.bfloat16)
    gate_grad = (hidden_grad * up_value * logistic * (1.0 + gate_value * (1.0 - logistic))).astype(
        jnp.bfloat16
    )
    return (hidden, gate_grad, up_grad)


def shards(tokens, cotangent, gate_weight, up_weight, down_weight):
    all_tokens, all_cotangent = (
        lax.all_gather(tokens, "out", axis=0, tiled=True),
        lax.all_gather(cotangent, "out", axis=0, tiled=True),
    )
    gate_full, up_full, down_full = (
        lax.all_gather(gate_weight, "dep", axis=0, tiled=True),
        lax.all_gather(up_weight, "dep", axis=0, tiled=True),
        lax.all_gather(down_weight, "dep", axis=0, tiled=True),
    )
    hidden_grad = contract_last(all_cotangent, down_full)
    gate_value = jnp.dot(all_tokens, gate_full, preferred_element_type=jnp.float32)
    up_value = jnp.dot(all_tokens, up_full, preferred_element_type=jnp.float32)
    gate_share, up_share, grad_share = (
        lax.psum_scatter(gate_value, "inp", scatter_dimension=1, tiled=True),
        lax.psum_scatter(up_value, "inp", scatter_dimension=1, tiled=True),
        lax.psum_scatter(hidden_grad, "inp", scatter_dimension=1, tiled=True),
    )
    hidden_share, gate_part, up_part = local_step(gate_share, up_share, grad_share)
    hidden, gate_grad, up_grad = (
        lax.all_gather(hidden_share, "inp", axis=1, tiled=True),
        lax.all_gather(gate_part, "inp", axis=1, tiled=True),
        lax.all_gather(up_part, "inp", axis=1, tiled=True),
    )
    input_terms = contract_last(gate_grad, gate_full) + contract_last(up_grad, up_full)
    token_grad = lax.psum_scatter(input_terms, "out", scatter_dimension=0, tiled=True)
    both_grads = jnp.concatenate((gate_grad, up_grad), axis=1)
    columns = gate_grad.shape[1]
    projection_total = lax.psum_scatter(
        contract_first(all_tokens, both_grads).astype(jnp.bfloat16),
        "dep",
        scatter_dimension=0,
        tiled=True,
    ).astype(jnp.float32)
    down_total = lax.psum_scatter(
        contract_first(hidden, all_cotangent).astype(jnp.bfloat16),
        "dep",
        scatter_dimension=0,
        tiled=True,
    ).astype(jnp.float32)
    gate_result = projection_total[:, :columns]
    up_result = projection_total[:, columns:]
    return (token_grad, gate_result, up_result, down_total)


def solution(mesh):
    return jax.shard_map(
        shards,
        mesh=mesh,
        in_specs=(
            P(("dep", "out"), "inp"),
            P(("dep", "out"), "inp"),
            P(("inp", "dep"), "out"),
            P(("inp", "dep"), "out"),
            P(("out", "dep"), "inp"),
        ),
        out_specs=(
            P(("dep", "out"), "inp"),
            P(("inp", "dep"), "out"),
            P(("inp", "dep"), "out"),
            P(("out", "dep"), "inp"),
        ),
        check_vma=False,
    )
```

profile of v0, /device:TPU:1, one launch (start us, length us, event | category | flops | bytes accessed | tf_op | source)
XLA Modules:
  0.0 536.5 jit_solution(109460322158937044)
XLA Ops:
  9.4 10.8 %all_gather.26 = bf16[128,512]{1,0:T(8,128)(2,1)S(1)} all-gather(bf16[32,512]{1,0:T(8,128)(2,1)} %param.5), channel_id=1, replica_groups=mesh['inp'=8,'out'=4,'dep'=8] {'out'}, dimensions={0}, use_global_device_ids=true | all-gather | bytes 163840 | tf_op jit(solution)/shard_map/all_gather | solution.py:32
  20.2 41.7 %all-gather.6.cloned.1.call-done = bf16[512,3584]{1,0:T(8,128)(2,1)} async-done(((bf16[64,3584]{1,0:T(8,128)(2,1)}), bf16[512,3584]{1,0:T(8,128)(2,1)}) %all-gather.6.cloned.1.call-update) | async-done | bytes 3670032 | tf_op jit(solution)/shard_map/all_gather | solution.py:37
  61.9 4.8 fusion.8
  66.8 43.9 %all-gather.8.cloned.1.call-done = bf16[512,3584]{1,0:T(8,128)(2,1)} async-done(((bf16[64,3584]{1,0:T(8,128)(2,1)}), bf16[512,3584]{1,0:T(8,128)(2,1)}) %all-gather.8.cloned.1.call-update) | async-done | bytes 3670032 | tf_op jit(solution)/shard_map/all_gather | solution.py:36
  110.7 4.8 fusion.9
  115.6 9.5 %all_gather.24 = bf16[128,512]{1,0:T(8,128)(2,1)S(1)} all-gather(bf16[32,512]{1,0:T(8,128)(2,1)S(1)} %copy-done.2), channel_id=1, replica_groups=mesh['inp'=8,'out'=4,'dep'=8] {'out'}, dimensions={0}, use_global_device_ids=true | all-gather | bytes 163840 | tf_op jit(solution)/shard_map/all_gather | solution.py:33
  125.1 34.3 %all-gather.4.cloned.1.call-done = bf16[3584,512]{1,0:T(8,128)(2,1)} async-done(((bf16[448,512]{1,0:T(8,128)(2,1)}), bf16[3584,512]{1,0:T(8,128)(2,1)}) %all-gather.4.cloned.1.call-update) | async-done | bytes 3670032 | tf_op jit(solution)/shard_map/all_gather | solution.py:38
  159.5 4.5 fusion.7
  164.0 35.5 %reduce-scatter.11.cloned.1.call-done = f32[128,448]{0,1:T(8,128)} async-done(((f32[128,3584]{0,1:T(8,128)}), f32[128,448]{0,1:T(8,128)}) %reduce-scatter.11.cloned.1.call-update) | async-done | bytes 229392 | tf_op jit(solution)/shard_map/reduce_scatter | solution.py:45
  199.5 46.1 %reduce-scatter.13.cloned.1.call-done = f32[128,448]{0,1:T(8,128)} async-done(((f32[128,3584]{0,1:T(8,128)}), f32[128,448]{0,1:T(8,128)}) %reduce-scatter.13.cloned.1.call-update) | async-done | bytes 229392 | tf_op jit(solution)/shard_map/reduce_scatter | solution.py:44
  245.6 45.9 %reduce-scatter.9.cloned.1.call-done = f32[128,448]{0,1:T(8,128)} async-done(((f32[128,3584]{0,1:T(8,128)}), f32[128,448]{0,1:T(8,128)}) %reduce-scatter.9.cloned.1.call-update) | async-done | bytes 229392 | tf_op jit(solution)/shard_map/reduce_scatter | solution.py:46
  292.8 23.1 %all_gather.31 = bf16[128,3584]{0,1:T(8,128)(2,1)S(1)} all-gather(bf16[128,448]{0,1:T(8,128)(2,1)S(1)} %get-tuple-element.14), channel_id=1, replica_groups=mesh['inp'=8,'out'=4,'dep'=8] {'inp'}, dimensions={1}, use_global_device_ids=true | all-gather | bytes 1032192 | tf_op jit(solution)/shard_map/all_gather | solution.py:50
  315.9 3.0 convolution_convert_fusion.1
  318.9 24.1 %all_gather.29 = bf16[128,3584]{0,1:T(8,128)(2,1)S(1)} all-gather(bf16[128,448]{0,1:T(8,128)(2,1)S(1)} %get-tuple-element.15), channel_id=1, replica_groups=mesh['inp'=8,'out'=4,'dep'=8] {'inp'}, dimensions={1}, use_global_device_ids=true | all-gather | bytes 1032192 | tf_op jit(solution)/shard_map/all_gather | solution.py:51
  343.0 35.2 %all_gather.30 = bf16[128,3584]{0,1:T(8,128)(2,1)S(1)} all-gather(bf16[128,448]{0,1:T(8,128)(2,1)S(1)} %get-tuple-element.16), channel_id=1, replica_groups=mesh['inp'=8,'out'=4,'dep'=8] {'inp'}, dimensions={1}, use_global_device_ids=true | all-gather | bytes 1032192 | tf_op jit(solution)/shard_map/all_gather | solution.py:52
  378.2 5.1 fusion
  383.2 10.1 %copy.13 = bf16[512,7168]{1,0:T(8,128)(2,1)} copy(bf16[512,7168]{0,1:T(8,128)(2,1)} %fusion) | data formatting | bytes 14680064
  393.4 3.5 fusion.10
  396.9 2.1 convolution_add_fusion
  399.0 2.1 convert_element_type.31
  401.1 104.3 %reduce-scatter.19.cloned.1.call-done = bf16[64,7168]{1,0:T(8,128)(2,1)} async-done(((bf16[512,7168]{1,0:T(8,128)(2,1)}), bf16[64,7168]{1,0:T(8,128)(2,1)}) %reduce-scatter.19.cloned.1.call-update) | async-done | bytes 917520
  507.3 2.0 fusion.6
  509.3 3.1 copy.11
  513.9 16.1 %reduce-scatter.15.cloned.1.call-done = f32[32,512]{1,0:T(8,128)} async-done(((f32[128,512]{1,0:T(8,128)}), f32[32,512]{1,0:T(8,128)}) %reduce-scatter.15.cloned.1.call-update) | async-done | bytes 65552 | tf_op jit(solution)/shard_map/reduce_scatter | solution.py:55
  (28 shorter events, 7.2 us)
Async XLA Ops:
  7.2 54.7 %all-gather.6.cloned.1.call-start = ((), (), s32[]{:S(2)}) async-start(), calls=%async_computation.8 | async-start | bytes 4128768 | tf_op jit(solution)/shard_map/all_gather | solution.py:37
  7.9 102.8 %all-gather.8.cloned.1.call-start = ((), (), s32[]{:S(2)}) async-start(), calls=%async_computation.10 | async-start | bytes 4128768 | tf_op jit(solution)/shard_map/all_gather | solution.py:36
  8.6 150.8 %all-gather.4.cloned.1.call-start = ((), (), s32[]{:S(2)}) async-start(), calls=%async_computation.6 | async-start | bytes 4128768 | tf_op jit(solution)/shard_map/all_gather | solution.py:38
  9.4 190.1 %reduce-scatter.11.cloned.1.call-start = ((), (), s32[]{:S(2)}) async-start(), calls=%async_computation.9 | async-start | bytes 2064384 | tf_op jit(solution)/shard_map/reduce_scatter | solution.py:45
  66.8 48.8 %copy-start.2 = (bf16[32,512]{1,0:T(8,128)(2,1)S(1)}, bf16[32,512]{1,0:T(8,128)(2,1)}, u32[]{:S(2)}) copy-start(bf16[32,512]{1,0:T(8,128)(2,1)} %param.6) | copy-start | bytes 98308
  66.8 178.8 %reduce-scatter.13.cloned.1.call-start = ((), (), s32[]{:S(2)}) async-start(), calls=%async_computation.11 | async-start | bytes 2064384 | tf_op jit(solution)/shard_map/reduce_scatter | solution.py:44
  115.5 175.9 %reduce-scatter.9.cloned.1.call-start = ((), (), s32[]{:S(2)}) async-start(), calls=%async_computation.7 | async-start | bytes 2064384 | tf_op jit(solution)/shard_map/reduce_scatter | solution.py:46
  164.0 235.1 %reduce-scatter.17.cloned.1.call-start = ((), (), s32[]{:S(2)}) async-start(), calls=%async_computation.13 | async-start | bytes 4128768 | tf_op jit(solution)/shard_map/reduce_scatter | solution.py:64
  318.9 186.5 %reduce-scatter.19.cloned.1.call-start = ((), (), s32[]{:S(2)}) async-start(), calls=%async_computation.14 | async-start | bytes 8257536
  393.3 136.6 %reduce-scatter.15.cloned.1.call-start = ((), (), s32[]{:S(2)}) async-start(), calls=%async_computation.12 | async-start | bytes 327680 | tf_op jit(solution)/shard_map/reduce_scatter | solution.py:55
  393.4 3.5 copy-start
  509.3 3.1 copy-start.1
Sparse Core Ops, SparseCore 0:
  9.8 52.0 all-gather.5
  63.7 46.9 all-gather.7
  112.5 46.9 all-gather.3
  161.9 37.5 reduce-scatter.10
  201.9 43.6 reduce-scatter.12
  248.0 43.4 reduce-scatter.8
  319.0 70.7 reduce-scatter.16
  393.4 111.8 reduce-scatter.18
  508.5 21.3 reduce-scatter.14
where the time goes:
time: 538 us; the launch traced here: 536 us
  waiting for transfers between devices  370 us (69%)
  blocking collectives  103 us (19%)
  matrix products  27.7 us (5%)
  local copies, waits for them, and re-layouts  18.6 us (3%)
  between operations  13.9 us (3%)
    unnamed x10, waiting for transfers between devices  106 us
    reduce_scatter x1, waiting for transfers between devices, shards(): lax.psum_scatter(gate_value, 'inp', scatter_dimension=1, tiled=True)  46.1 us
    reduce_scatter x1, waiting for transfers between devices, shards(): lax.psum_scatter(hidden_grad, 'inp', scatter_dimension=1, tiled=True)  45.9 us
    all_gather x1, waiting for transfers between devices, shards(): lax.all_gather(gate_weight, 'dep', axis=0, tiled=True)  43.9 us
    all_gather x1, waiting for transfers between devices, shards(): lax.all_gather(up_weight, 'dep', axis=0, tiled=True)  41.7 us
    reduce_scatter x1, waiting for transfers between devices, shards(): lax.psum_scatter(up_value, 'inp', scatter_dimension=1, tiled=True)  35.5 us
    all_gather x1, blocking collectives, shards(): lax.all_gather(up_part, 'inp', axis=1, tiled=True)  35.2 us
    all_gather x1, waiting for transfers between devices, shards(): lax.all_gather(down_weight, 'dep', axis=0, tiled=True)  34.3 us
  transfers between devices with their start and end apart: 9, of which 8 were waited for; matrix products, arithmetic and copies ran while one was open for 8% of the time, Pallas kernels for 0%

commit v1 on v0

v1 whole, which is shorter than its diff:
```python
import jax
import jax.numpy as jnp
from jax import lax
from jax.sharding import PartitionSpec as P


def contract_last(left_side, right_side):
    return lax.dot_general(
        left_side, right_side, (((1,), (1,)), ((), ())), preferred_element_type=jnp.float32
    )


def contract_first(left_side, right_side):
    return lax.dot_general(
        left_side, right_side, (((0,), (0,)), ((), ())), preferred_element_type=jnp.float32
    )


def local_step(gate_value, up_value, hidden_grad):
    logistic = jax.nn.sigmoid(gate_value)
    activated = gate_value * logistic
    hidden = (activated * up_value).astype(jnp.bfloat16)
    up_grad = (hidden_grad * activated).astype(jnp.bfloat16)
    gate_grad = (hidden_grad * up_value * logistic * (1.0 + gate_value * (1.0 - logistic))).astype(
        jnp.bfloat16
    )
    return (hidden, gate_grad, up_grad)


def shards(tokens, cotangent, gate_weight, up_weight, down_weight):
    n_inp = lax.axis_size("inp")
    both = jnp.concatenate((tokens, cotangent), axis=1)
    both = lax.all_gather(both, ("dep", "out"), axis=0, tiled=True)
    width = tokens.shape[1]
    all_tokens, all_cotangent = both[:, :width], both[:, width:]
    weights = jnp.stack((gate_weight, up_weight))
    weights = lax.all_to_all(weights, "dep", split_axis=2, concat_axis=1, tiled=True)
    gate_block, up_block = weights[0], weights[1]
    gate_value = jnp.dot(all_tokens, gate_block, preferred_element_type=jnp.float32)
    up_value = jnp.dot(all_tokens, up_block, preferred_element_type=jnp.float32)
    hidden_grad = contract_last(all_cotangent, down_weight)
    parts = jnp.stack((gate_value, up_value, hidden_grad)).astype(jnp.bfloat16)
    rows, columns = gate_value.shape
    parts = parts.reshape(3, n_inp, rows // n_inp, columns)
    parts = lax.all_to_all(parts, "inp", split_axis=1, concat_axis=1, tiled=True)
    sums = jnp.sum(parts.astype(jnp.float32), axis=1)
    shares = jnp.stack(local_step(sums[0], sums[1], sums[2]))
    full = lax.all_gather(shares, "inp", axis=1, tiled=True)
    hidden, gate_grad, up_grad = full[0], full[1], full[2]
    input_terms = contract_last(gate_grad, gate_block) + contract_last(up_grad, up_block)
    token_grad = lax.psum_scatter(input_terms, ("dep", "out"), scatter_dimension=0, tiled=True)
    grads = jnp.stack(
        (contract_first(all_tokens, gate_grad), contract_first(all_tokens, up_grad))
    ).astype(jnp.bfloat16)
    grads = lax.all_to_all(grads, "dep", split_axis=1, concat_axis=2, tiled=True)
    grads = grads.astype(jnp.float32)
    down_total = contract_first(hidden, all_cotangent)
    return (token_grad, grads[0], grads[1], down_total)


def solution(mesh):
    return jax.shard_map(
        shards,
        mesh=mesh,
        in_specs=(
            P(("dep", "out"), "inp"),
            P(("dep", "out"), "inp"),
            P(("inp", "dep"), "out"),
            P(("inp", "dep"), "out"),
            P(("out", "dep"), "inp"),
        ),
        out_specs=(
            P(("dep", "out"), "inp"),
            P(("inp", "dep"), "out"),
            P(("inp", "dep"), "out"),
            P(("out", "dep"), "inp"),
        ),
        check_vma=False,
    )
```

time: 538 us -> 273 us (0.51)
  waiting for transfers between devices: 370 us -> 133 us
  blocking collectives: 103 us -> 74.6 us
  matrix products: 27.7 us -> 15.3 us
  starting transfers between devices: 0.36 us -> 10.8 us
    unnamed x10 -> x3, waiting for transfers between devices: 106 us -> 0.05 us
    all_gather x5 -> x0, blocking collectives: 103 us -> none  [the longest x1 35.2 us: shards(): lax.all_gather(up_part, 'inp', axis=1, tiled=True)]
    reduce_scatter x5 -> x1, waiting for transfers between devices: 144 us -> 45 us  [shards(): lax.psum_scatter(input_terms, ('dep', 'out'), scatter_dimension=0, tiled=...]
    all_to_all x0 -> x2, blocking collectives: none -> 74.6 us  [the longest x1 37.7 us: shards(): lax.all_to_all(weights, 'dep', split_axis=2, concat_axis=1, tiled=True)]
    all_gather x3 -> x2, waiting for transfers between devices: 120 us -> 64.3 us  [the longest x1 45.3 us: shards(): full = lax.all_gather(shares, 'inp', axis=1, tiled=True)]
    all_to_all x0 -> x1, waiting for transfers between devices: none -> 23.2 us  [shards(): lax.all_to_all(grads, 'dep', split_axis=1, concat_axis=2, tiled=True)]
    all_to_all x0 -> x1, starting transfers between devices: none -> 10.7 us  [shards(): lax.all_to_all(grads, 'dep', split_axis=1, concat_axis=2, tiled=True)]
    dot_general x2, matrix products: 9.66 us -> 1.39 us  [the longest x1 0.7 us: shards(): jnp.dot(all_tokens, gate_block, preferred_element_type=jnp.float32)]
  transfers between devices with their start and end apart: 9 -> 4, of which waited for: 8 -> 4; matrix products, arithmetic and copies ran while one was open for 8% -> 9% of each run, Pallas kernels for 0% -> 0%
where the time goes in v1:
time: 273 us; the launch traced here: 271 us
  waiting for transfers between devices  133 us (49%)
  blocking collectives  74.6 us (27%)
  local copies, waits for them, and re-layouts  19.6 us (7%)
  matrix products  15.3 us (6%)
  between operations  13.9 us (5%)
  starting transfers between devices  10.8 us (4%)
  other arithmetic  4.69 us (2%)
    all_gather x1, waiting for transfers between devices, shards(): full = lax.all_gather(shares, 'inp', axis=1, tiled=True)  45.3 us
    reduce_scatter x1, waiting for transfers between devices, shards(): lax.psum_scatter(input_terms, ('dep', 'out'), scatter_dimension=0, tiled=...  45 us
    all_to_all x1, blocking collectives, shards(): lax.all_to_all(weights, 'dep', split_axis=2, concat_axis=1, tiled=True)  37.7 us
    all_to_all x1, blocking collectives, shards(): lax.all_to_all(parts, 'inp', split_axis=1, concat_axis=1, tiled=True)  36.9 us
    all_to_all x1, waiting for transfers between devices, shards(): lax.all_to_all(grads, 'dep', split_axis=1, concat_axis=2, tiled=True)  23.2 us
    all_gather x1, waiting for transfers between devices, shards(): both = lax.all_gather(both, ('dep', 'out'), axis=0, tiled=True)  19 us
    all_to_all x1, starting transfers between devices, shards(): lax.all_to_all(grads, 'dep', split_axis=1, concat_axis=2, tiled=True)  10.7 us
    unnamed x9, local copies, waits for them, and re-layouts  8.85 us
  transfers between devices with their start and end apart: 4, of which 4 were waited for; matrix products, arithmetic and copies ran while one was open for 9% of the time, Pallas kernels for 0%

profile of v1, /device:TPU:1, one launch (start us, length us, event | category | flops | bytes accessed | tf_op | source)
XLA Modules:
  0.0 271.4 jit_solution(9840788655675022764)
XLA Ops:
  7.2 1.5 pad_maximum_fusion.4
  8.8 1.2 pad_maximum_fusion.1
  10.0 2.5 copy.36
  12.5 1.3 reshape.43
  13.9 37.7 %all_to_all.29 = bf16[8,2,28672]{2,1,0:T(2,128)(2,1)} all-to-all(bf16[8,2,28672]{2,1,0:T(2,128)(2,1)S(1)} %reshape.43), channel_id=1, replica_groups=mesh['inp'=8,'out'=4,'dep'=8] {'dep'}, dimensions={0} | all-to-all | bytes 1835008 | tf_op jit(solution)/shard_map/all_to_all | solution.py:37
  51.5 4.5 %reshape.44 = bf16[3584,2,64]{2,1,0:T(2,128)(2,1)S(1)} reshape(bf16[8,2,28672]{2,1,0:T(2,128)(2,1)} %all_to_all.29) | data formatting | bytes 1835008
  56.0 1.4 copy.37
  57.5 19.0 %all-gather.3.cloned.1.call-done = bf16[1024,1024]{1,0:T(8,128)(2,1)} async-done(((bf16[32,1024]{1,0:T(8,128)(2,1)}), bf16[1024,1024]{1,0:T(8,128)(2,1)}) %all-gather.3.cloned.1.call-update) | async-done | bytes 2097168 | tf_op jit(solution)/shard_map/all_gather | solution.py:33
  76.5 1.9 fusion.2
  78.8 1.2 copy-done.1
  82.0 36.9 %all_to_all.30 = bf16[3,8,128,448]{2,3,0,1:T(8,128)(2,1)S(1)} all-to-all(bf16[3,8,128,448]{2,3,0,1:T(8,128)(2,1)S(1)} %copy.41), channel_id=1, replica_groups=mesh['inp'=8,'out'=4,'dep'=8] {'inp'}, dimensions={1} | all-to-all | bytes 5505024 | tf_op jit(solution)/shard_map/all_to_all | solution.py:45
  120.4 45.3 %all-gather.5.cloned.1.call-done = bf16[3,1024,448]{1,2,0:T(8,128)(2,1)} async-done(((bf16[3,128,448]{1,2,0:T(8,128)(2,1)}), bf16[3,1024,448]{1,2,0:T(8,128)(2,1)}) %all-gather.5.cloned.1.call-update) | async-done | bytes 2752528 | tf_op jit(solution)/shard_map/all_gather | solution.py:48
  165.6 1.9 fusion.8
  167.6 3.3 %convolution_add_fusion = f32[1024,512]{1,0:T(8,128)} fusion(f32[1024,512]{1,0:T(8,128)S(1)} %fusion.8, bf16[512,448]{1,0:T(8,128)(2,1)S(1)} %bitcast.61, bf16[3,1024,448]{1,2,0:T(8,128)(2,1)} %all-gather.5.cloned.1.call-done), kind=kOutput, calls=%fused_computation.3 | convolution fusion | flops 470286336 | bytes 5570560 | tf_op jit(solution)/shard_map/dot_general | solution.py:8
  170.9 1.6 copy-done.2
  172.5 1.8 fusion.4
  174.3 1.8 fusion.3
  176.3 2.1 copy.43
  178.4 10.7 %all-to-all-start.2 = ((bf16[2,512,448]{2,0,1:T(2,128)(2,1)}), bf16[2,512,448]{2,0,1:T(2,128)(2,1)S(1)}, u32[]{:S(2)}, u32[]{:S(2)}) async-start(bf16[2,512,448]{2,0,1:T(2,128)(2,1)} %copy.43), calls=%async_computation.3 | async-start | bytes 2097152 | tf_op jit(solution)/shard_map/all_to_all | solution.py:55
  189.0 3.1 %fusion.5 = f32[448,512]{1,0:T(8,128)} fusion(bf16[1024,1024]{1,0:T(8,128)(2,1)} %all-gather.3.cloned.1.call-done, bf16[3,1024,448]{1,2,0:T(8,128)(2,1)} %all-gather.5.cloned.1.call-done), kind=kOutput, calls=%fused_computation.14 | convolution fusion | flops 469762048 | bytes 2883584 | tf_op jit(solution)/shard_map/dot_general | solution.py:14
  192.1 23.2 %all-to-all-done.2 = bf16[2,512,448]{2,0,1:T(2,128)(2,1)S(1)} async-done(((bf16[2,512,448]{2,0,1:T(2,128)(2,1)}), bf16[2,512,448]{2,0,1:T(2,128)(2,1)S(1)}, u32[]{:S(2)}, u32[]{:S(2)}) %all-to-all-start.2) | async-done | bytes 917536 | tf_op jit(solution)/shard_map/all_to_all | solution.py:55
  216.6 1.3 squeeze.29
  218.5 1.3 squeeze.28
  219.9 45.0 %reduce-scatter.2.cloned.1.call-done = f32[32,512]{1,0:T(8,128)} async-done(((f32[1024,512]{1,0:T(8,128)}), f32[32,512]{1,0:T(8,128)}) %reduce-scatter.2.cloned.1.call-update) | async-done | bytes 65552 | tf_op jit(solution)/shard_map/reduce_scatter | solution.py:51
  (27 shorter events, 5.9 us)
Async XLA Ops:
  7.2 69.4 %copy-start = (bf16[448,512]{1,0:T(8,128)(2,1)S(1)}, bf16[448,512]{1,0:T(8,128)(2,1)}, u32[]{:S(2)}) copy-start(bf16[448,512]{1,0:T(8,128)(2,1)} %param.9) | copy-start | bytes 1376260
  7.2 69.3 %all-gather.3.cloned.1.call-start = ((), (), s32[]{:S(2)}) async-start(), calls=%async_computation.4 | async-start | bytes 2162688 | tf_op jit(solution)/shard_map/all_gather | solution.py:33
  8.7 156.9 %all-gather.5.cloned.1.call-start = ((), (), s32[]{:S(2)}) async-start(), calls=%async_computation.5 | async-start | bytes 3096576 | tf_op jit(solution)/shard_map/all_gather | solution.py:48
  78.4 1.6 copy-start.1
  120.3 144.6 %reduce-scatter.2.cloned.1.call-start = ((), (), s32[]{:S(2)}) async-start(), calls=%async_computation.6 | async-start | bytes 2162688 | tf_op jit(solution)/shard_map/reduce_scatter | solution.py:51
  170.9 1.6 copy-start.2
  178.4 37.0 %all-to-all-start.2 = ((bf16[2,512,448]{2,0,1:T(2,128)(2,1)}), bf16[2,512,448]{2,0,1:T(2,128)(2,1)S(1)}, u32[]{:S(2)}, u32[]{:S(2)}) async-start(bf16[2,512,448]{2,0,1:T(2,128)(2,1)} %copy.43), calls=%async_computation.3 | async-start | bytes 2097152 | tf_op jit(solution)/shard_map/all_to_all | solution.py:55
Sparse Core Ops, SparseCore 0:
  11.1 65.3 all-gather.2
  120.4 45.1 all-gather.4
  171.1 93.7 reduce-scatter.1

commit v2 on v1

v2 whole, which is shorter than its diff:
```python
import jax
import jax.numpy as jnp
from jax import lax
from jax.experimental import pallas as pl
from jax.experimental.pallas import tpu as pltpu
from jax.sharding import PartitionSpec as P

F32, BF16 = jnp.float32, jnp.bfloat16
MESH = pl.DeviceIdType.MESH
NX, NY, NZH = 4, 4, 4
SUB = 112
HALF = 512
COPIES = 160


def nt(left_side, right_side):
    return lax.dot_general(left_side, right_side, (((1,), (1,)), ((), ())), preferred_element_type=F32)


def nn(left_side, right_side):
    return jnp.dot(left_side, right_side, preferred_element_type=F32)


def tn(left_side, right_side):
    return lax.dot_general(left_side, right_side, (((0,), (0,)), ((), ())), preferred_element_type=F32)


def local_step(gate_value, up_value, hidden_grad):
    logistic = 1.0 / (1.0 + jnp.exp(-gate_value))
    activated = gate_value * logistic
    hidden = (activated * up_value).astype(BF16)
    up_grad = (hidden_grad * activated).astype(BF16)
    gate_grad = (hidden_grad * up_value * logistic * (1.0 + gate_value * (1.0 - logistic))).astype(BF16)
    return (hidden, gate_grad, up_grad)


def lanes(block):
    return pl.ds(pl.multiple_of(block * 128, 128), 128)


def kernel(
    tok_in, cot_in, gate_in, up_in, down_in,
    tg_out, gate_out, up_out, down_out,
    wt, wblk, gu, tok, cot, rs_send, rs_recv, hg_send, hg_recv, hz_send, hz_recv,
    grads, hid, wg_send, wg_recv, ta_send, ta_recv, tb_send, tb_recv, tc_send, tc_recv, td_send, td_recv,
    send_sems, recv_sems,
):
    inp, y, dep = lax.axis_index("inp"), lax.axis_index("out"), lax.axis_index("dep")
    zl, x = inp // NX, inp % NX
    zh, c = dep // 2, dep % 2
    z = zh * 2 + zl

    def at(x_=x, y_=y, zh_=zh, zl_=zl, c_=c):
        return (zl_ * NX + x_, y_, zh_ * 2 + c_)

    def ring(step):
        there = (z + step + 8) % 8
        return (there // 2, there % 2)

    xs = [(x + k) % NX for k in range(NX)]
    ys = [(y + k) % NY for k in range(NY)]
    zhs = [(zh + k) % NZH for k in range(NZH)]
    cs = [c, 1 - c]
    sides = [ring(1), ring(-1)]
    around = [at(zh_=side[0], zl_=side[1]) for side in sides]
    partner = at(zl_=1 - zl)

    peers = [at(c_=cs[1])]
    peers += [at(x_=xs[k], c_=cs[e]) for k in range(1, NX) for e in range(2)]
    peers += [at(x_=xs[k], zh_=zhs[m]) for k in range(NX) for m in range(1, NZH)]
    peers += [at(y_=ys[k]) for k in range(1, NY)]
    peers += around
    barrier = pltpu.get_barrier_semaphore()
    for peer in peers:
        pl.semaphore_signal(barrier, inc=1, device_id=peer, device_id_type=MESH)

    for q in range(NZH):
        columns = pl.ds(q * 896, 896)
        both = jnp.concatenate((gate_in[:, columns], up_in[:, columns]), axis=0)
        wt[q] = both.T.reshape(2, NX, SUB, 128)
    wblk[x * 2 + c] = wt[:, c, x]
    tok[zh, c, y, :, lanes(x)] = tok_in[:, lanes(zh)]
    cot[zh, c, y] = cot_in[...]

    pl.semaphore_wait(barrier, len(peers))

    started = []

    def send(src, dst, device):
        index = len(started)
        copy = pltpu.make_async_remote_copy(
            src_ref=src, dst_ref=dst, send_sem=send_sems.at[index], recv_sem=recv_sems.at[index],
            device_id=device, device_id_type=MESH,
        )
        copy.start()
        started.append(copy)
        return copy

    def arrive(copies):
        for copy in copies:
            copy.wait_recv()

    tok_first = [
        send(tok_in.at[:, lanes(zhs[m])], tok.at[zh, c, y, :, lanes(x)], at(x_=xs[k], zh_=zhs[m]))
        for m in range(NZH) for k in range(NX) if (m, k) != (0, 0)
    ]
    cot_first = [send(cot_in, cot.at[zh, c, y], at(zh_=zhs[m])) for m in range(1, NZH)]
    order = [zhs[2], zhs[1], zhs[3], zhs[0]]
    weights = [
        [
            send(wt.at[q, cs[e], xs[k]], wblk.at[x * 2 + c, q], at(x_=xs[k], c_=cs[e]))
            for k in range(NX) for e in range(2) if (k, e) != (0, 0)
        ]
        for q in order
    ]

    def spread(buffer, first):
        arrive(first)
        own = buffer.at[:, c, y]
        return [send(own, own, at(y_=ys[k])) for k in range(1, NY)], [send(own, own, at(c_=cs[1]))]

    def share(buffer, by_y, by_core):
        for k in range(1, NY):
            by_y[k - 1].wait_recv()
            rows = buffer.at[:, c, ys[NY - k]]
            by_core.append(send(rows, rows, at(c_=cs[1])))

    tok_y, tok_core = spread(tok, tok_first)
    cot_y, cot_core = spread(cot, cot_first)

    def assemble(q, copies):
        arrive(copies)
        for k in range(NX):
            even, odd = wblk[2 * k, q], wblk[2 * k + 1, q]
            here = pl.ds(k * 128, 128)
            gu[0, q, :, here] = jnp.concatenate((even[:, :64], odd[:, :64]), axis=1)
            gu[1, q, :, here] = jnp.concatenate((even[:, 64:], odd[:, 64:]), axis=1)

    assemble(order[0], weights[0])
    share(tok, tok_y, tok_core)
    arrive(tok_core)

    def partial(there):
        rows = gu[:, there[0]].reshape(2 * SUB, HALF)
        seen = tok[pl.ds(there[1] * 2, 2)].reshape(HALF, HALF)
        return nt(rows, seen).reshape(2, SUB, HALF)

    halves = [pl.ds(0, 256), pl.ds(256, 256)]
    own = partial(ring(4))
    rs_send[:, 0] = jnp.stack((own, own)).astype(BF16)
    moving = [
        [send(rs_send.at[d, 0, m, :, halves[d]], rs_recv.at[d, 0, m, :, halves[d]], around[d]) for d in range(2)]
        for m in range(2)
    ]

    for q in range(1, NZH):
        assemble(order[q], weights[q])
    share(cot, cot_y, cot_core)

    def onward(step, moving):
        terms = [partial(ring(4 - step)), partial(ring(step - 4))]
        later = []
        for m in range(2):
            row = []
            for d in range(2):
                moving[m][d].wait_recv()
                if step == 1:
                    came = rs_recv[d, 0, m, :, halves[d]].astype(F32)
                    parts = [terms[d][m][:, :256], terms[d][m][:, 256:]]
                    parts[d] = parts[d] + came
                    total = jnp.concatenate(parts, axis=1)
                else:
                    total = terms[d][m] + rs_recv[d, step - 1, m].astype(F32)
                rs_send[d, step, m] = total.astype(BF16)
                row.append(send(rs_send.at[d, step, m], rs_recv.at[d, step, m], around[d]))
            later.append(row)
        return later

    moving = onward(1, moving)

    arrive(cot_core)
    all_cot = cot[...].reshape(2 * HALF, HALF)

    def hidden_part(q):
        rows = down_in[pl.ds(pl.multiple_of(q * SUB, 16), SUB), :]
        return nt(rows, all_cot)

    by_x = []
    for k in range(1, NX):
        part = hidden_part(xs[k]).astype(BF16)
        hg_send[k - 1, 0] = part[:, :HALF]
        hg_send[k - 1, 1] = part[:, HALF:]
        by_x.append(send(hg_send.at[k - 1], hg_recv.at[k - 1], at(x_=xs[k])))
    moving = onward(2, moving)
    own = hidden_part(x)
    hz_send[0] = own[:, :HALF]
    hz_send[1] = own[:, HALF:]
    arrive(by_x)

    def hidden_sum(half):
        total = hz_send[half]
        for k in range(NX - 1):
            total = total + hg_recv[k, half].astype(F32)
        return total

    hz_recv[0] = hidden_sum(1 - zl).astype(BF16)
    by_pair = send(hz_recv.at[0], hz_recv.at[1], partner)
    moving = onward(3, moving)
    hidden_grad = hidden_sum(zl)
    by_pair.wait_recv()
    hidden_grad = hidden_grad + hz_recv[1].astype(F32)
    values = partial((zh, zl))
    sums = []
    for m in range(2):
        total = values[m]
        for d in range(2):
            moving[m][d].wait_recv()
            total = total + rs_recv[d, 3, m].astype(F32)
        sums.append(total)
    hidden, gate_grad, up_grad = local_step(sums[0], sums[1], hidden_grad)

    grads[zl, 0, zh] = gate_grad
    grads[zl, 1, zh] = up_grad

    def chunk(there, m, step, d):
        if step == 3:
            return grads.at[there[1], m, there[0], :, halves[d]]
        return grads.at[there[1], m, there[0]]

    def forward(step):
        rows = []
        for m in range(2):
            row = []
            for d in range(2):
                block = chunk(ring(-step if d == 0 else step), m, step, d)
                row.append(send(block, block, around[d]))
            rows.append(row)
        return rows

    moving = forward(0)
    hid[zl, x] = hidden
    by_pair = send(hid.at[zl, x], hid.at[zl, x], partner)
    by_pair.wait_recv()
    by_x = [send(hid.at[:, x], hid.at[:, x], at(x_=xs[k])) for k in range(1, NX)]

    returned = []

    def weight_grads(q):
        both = []
        for m in range(2):
            both.append(
                nn(grads[0, m, q], tok[0:2].reshape(HALF, HALF))
                + nn(grads[1, m, q], tok[2:4].reshape(HALF, HALF))
            )
        both = [one.astype(BF16) for one in both]
        for k in range(NX):
            here = [one[:, k * 128 : (k + 1) * 128] for one in both]
            wg_send[q, 0, k] = jnp.concatenate((here[0][:, :64], here[1][:, :64]), axis=1)
            wg_send[q, 1, k] = jnp.concatenate((here[0][:, 64:], here[1][:, 64:]), axis=1)
        wg_recv[q, c, x] = wg_send[q, c, x]
        for k in range(NX):
            for e in range(2):
                if (k, e) != (0, 0):
                    returned.append(
                        send(wg_send.at[q, cs[e], xs[k]], wg_recv.at[q, c, x], at(x_=xs[k], c_=cs[e]))
                    )

    turn = 2 * zl - 1
    finished = [zh, (zh + turn + NZH) % NZH, (zh - turn + NZH) % NZH, zhs[2]]
    for step in range(4):
        later = []
        for m in range(2):
            arrive(moving[m])
            if step < 3:
                row = []
                for d in range(2):
                    block = chunk(ring(-step - 1 if d == 0 else step + 1), m, step + 1, d)
                    row.append(send(block, block, around[d]))
                later.append(row)
        moving = later
        if step < 3:
            weight_grads(finished[step])
        if step == 1:
            arrive(by_x)
            for q in range(NX):
                down_out[pl.ds(q * SUB, SUB), :] = nn(
                    hid[0, q], cot[0:2].reshape(HALF, HALF)
                ) + nn(hid[1, q], cot[2:4].reshape(HALF, HALF))

    terms = []
    for half in range(2):
        term = tn(grads[half].reshape(8 * SUB, HALF), gu[...].reshape(8 * SUB, HALF))
        terms.append(term.reshape(2, 2, NY, 32, HALF))
    ta_all = jnp.concatenate(terms, axis=0)
    tb_send[...] = ta_all
    ta_send[...] = tb_send[:, cs[1]].astype(BF16)
    by_core = send(ta_send, ta_recv, at(c_=cs[1]))
    weight_grads(finished[3])
    by_core.wait_recv()
    ta_send_sum = tb_send[:, c] + ta_recv[...].astype(F32)
    tb_send[:, c] = ta_send_sum
    for k in range(NX):
        tb_recv[0, k] = ta_send_sum[:, :, :, k * 128 : (k + 1) * 128].astype(BF16)
    by_x = [send(tb_recv.at[0, xs[k]], tb_recv.at[1, k], at(x_=xs[k])) for k in range(1, NX)]
    total = tb_send[:, c, :, :, lanes(x)]
    arrive(by_x)
    for k in range(1, NX):
        total = total + tb_recv[1, k].astype(F32)
    tc_send[...] = total
    for k in range(NY):
        tc_recv[0, k] = total[:, k].astype(BF16)
    by_y = [send(tc_recv.at[0, ys[k]], tc_recv.at[1, k], at(y_=ys[k])) for k in range(1, NY)]
    total = tc_send[:, y]
    arrive(by_y)
    for k in range(1, NY):
        total = total + tc_recv[1, k].astype(F32)
    td_send[...] = total
    td_recv[zh] = td_send[zh]
    by_z = [send(td_send.at[zhs[m]], td_recv.at[zh], at(zh_=zhs[m])) for m in range(1, NZH)]

    arrive(returned)
    for q in range(NZH):
        block = wg_recv[q].reshape(896, 128).T.astype(F32)
        gate_out[:, pl.ds(q * 896, 896)] = block[:64]
        up_out[:, pl.ds(q * 896, 896)] = block[64:]
    arrive(by_z)
    for q in range(NZH):
        tg_out[:, pl.ds(q * 128, 128)] = td_recv[q]
    for copy in started:
        copy.wait_send()


def shards(tokens, cotangent, gate_weight, up_weight, down_weight):
    vmem = pl.BlockSpec(memory_space=pltpu.VMEM)
    outs = [
        jax.ShapeDtypeStruct(tokens.shape, F32),
        jax.ShapeDtypeStruct(gate_weight.shape, F32),
        jax.ShapeDtypeStruct(up_weight.shape, F32),
        jax.ShapeDtypeStruct(down_weight.shape, F32),
    ]
    scratch = [
        pltpu.VMEM((NZH, 2, NX, SUB, 128), BF16),
        pltpu.VMEM((2 * NX, NZH, SUB, 128), BF16),
        pltpu.VMEM((2, NZH, SUB, HALF), BF16),
        pltpu.VMEM((NZH, 2, NY, 32, HALF), BF16),
        pltpu.VMEM((NZH, 2, NY, 32, HALF), BF16),
        pltpu.VMEM((2, 4, 2, SUB, HALF), BF16),
        pltpu.VMEM((2, 4, 2, SUB, HALF), BF16),
        pltpu.VMEM((NX - 1, 2, SUB, HALF), BF16),
        pltpu.VMEM((NX - 1, 2, SUB, HALF), BF16),
        pltpu.VMEM((2, SUB, HALF), F32),
        pltpu.VMEM((2, SUB, HALF), BF16),
        pltpu.VMEM((2, 2, NZH, SUB, HALF), BF16),
        pltpu.VMEM((2, NX, SUB, HALF), BF16),
        pltpu.VMEM((NZH, 2, NX, SUB, 128), BF16),
        pltpu.VMEM((NZH, 2, NX, SUB, 128), BF16),
        pltpu.VMEM((NZH, NY, 32, HALF), BF16),
        pltpu.VMEM((NZH, NY, 32, HALF), BF16),
        pltpu.VMEM((NZH, 2, NY, 32, HALF), F32),
        pltpu.VMEM((2, NX, NZH, NY, 32, 128), BF16),
        pltpu.VMEM((NZH, NY, 32, 128), F32),
        pltpu.VMEM((2, NY, NZH, 32, 128), BF16),
        pltpu.VMEM((NZH, 32, 128), F32),
        pltpu.VMEM((NZH, 32, 128), F32),
        pltpu.SemaphoreType.DMA((COPIES,)),
        pltpu.SemaphoreType.DMA((COPIES,)),
    ]
    return pl.pallas_call(
        kernel,
        out_shape=outs,
        in_specs=[vmem] * 5,
        out_specs=[vmem] * 4,
        scratch_shapes=scratch,
        compiler_params=pltpu.CompilerParams(
            collective_id=0, has_side_effects=True, vmem_limit_bytes=52 * 2**20
        ),
        name="layer",
    )(tokens, cotangent, gate_weight, up_weight, down_weight)


def solution(mesh):
    return jax.shard_map(
        shards,
        mesh=mesh,
        in_specs=(
            P(("dep", "out"), "inp"),
            P(("dep", "out"), "inp"),
            P(("inp", "dep"), "out"),
            P(("inp", "dep"), "out"),
            P(("out", "dep"), "inp"),
        ),
        out_specs=(
            P(("dep", "out"), "inp"),
            P(("inp", "dep"), "out"),
            P(("inp", "dep"), "out"),
            P(("out", "dep"), "inp"),
        ),
        check_vma=False,
    )
```

time: 273 us -> 118 us (0.43)
  waiting for transfers between devices: 133 us -> 0 us
  Pallas kernels: 0 us -> 107 us
  blocking collectives: 74.6 us -> 0 us
  matrix products: 15.3 us -> 0 us
  between operations: 13.9 us -> 0.66 us
  starting transfers between devices: 10.8 us -> 0 us
  local copies, waits for them, and re-layouts: 19.6 us -> 9.88 us
  other arithmetic: 4.69 us -> 0 us
    pallas_call x0 -> x1, Pallas kernels: none -> 107 us  [shards(): pl.pallas_call(kernel, out_shape=outs, in_specs=[vmem] * 5, out_specs=[vm...]
    all_to_all x2 -> x0, blocking collectives: 74.6 us -> none  [the longest x1 37.7 us: shards(): lax.all_to_all(weights, 'dep', split_axis=2, concat_axis=1, tiled=True)]
    all_gather x2 -> x0, waiting for transfers between devices: 64.3 us -> none  [the longest x1 45.3 us: shards(): full = lax.all_gather(shares, 'inp', axis=1, tiled=True)]
    reduce_scatter x1 -> x0, waiting for transfers between devices: 45 us -> none  [shards(): lax.psum_scatter(input_terms, ('dep', 'out'), scatter_dimension=0, tiled=...]
    all_to_all x1 -> x0, waiting for transfers between devices: 23.2 us -> none  [shards(): lax.all_to_all(grads, 'dep', split_axis=1, concat_axis=2, tiled=True)]
    dot_general x8 -> x0, matrix products: 15.3 us -> none  [the longest x3 7.16 us: contract_last(): lax.dot_general(left_side, right_side, (((1,), (1,)), ((), ())), preferre...]
    all_to_all x1 -> x0, starting transfers between devices: 10.7 us -> none  [shards(): lax.all_to_all(grads, 'dep', split_axis=1, concat_axis=2, tiled=True)]
    another operation x4 -> x0, local copies, waits for them, and re-layouts: 4.91 us -> none  [the longest x1 2.5 us: shards(): weights = jnp.stack((gate_weight, up_weight))]
  transfers between devices with their start and end apart: 4 -> 0, of which waited for: 4 -> 0; matrix products, arithmetic and copies ran while one was open for 9% -> 0% of each run, Pallas kernels for 0% -> 0%
where the time goes in v2:
time: 118 us; the launch traced here: 117 us
  Pallas kernels  107 us (91%)
  local copies, waits for them, and re-layouts  9.88 us (8%)
    pallas_call x1, Pallas kernels, shards(): pl.pallas_call(kernel, out_shape=outs, in_specs=[vmem] * 5, out_specs=[vm...  107 us
    unnamed x18, local copies, waits for them, and re-layouts  9.88 us

profile of v2, /device:TPU:1, one launch (start us, length us, event | category | flops | bytes accessed | tf_op | source)
XLA Modules:
  0.0 117.3 jit_solution(13724067379634775746)
XLA Ops:
  0.6 0.0 copy-start
  0.6 1.0 copy-done
  1.7 0.0 copy-start.1
  1.7 1.0 copy-done.1
  2.7 0.0 copy-start.2
  2.7 1.0 copy-done.2
  3.7 0.0 copy-start.3
  3.7 0.8 copy-done.3
  4.4 0.0 copy-start.4
  4.5 0.8 copy-done.4
  5.2 106.7 %layer.1 = (f32[32,512]{1,0:T(8,128)S(1)}, f32[64,3584]{1,0:T(8,128)}, f32[64,3584]{1,0:T(8,128)}, f32[448,512]{1,0:T(8,128)}) custom-call(bf16[32,512]{1,0:T(8,128)(2,1)S(1)} %copy-done.3, bf16[32,512]{1,0:T(8,128)(2,1)S(1)} %copy-done.4, bf16[64,3584]{1,0:T(8,128)(2,1)S(1)} %copy-done, bf16[64,3584]{1,0:T(8,128)(2,1)S(1)} %copy-done.1, ...), custom_call_target="tpu_custom_call" | custom-call | tf_op jit(solution)/shard_map/layer/pallas_call | solution.py:368
  112.0 0.6 copy.13
  112.6 0.0 copy-start.6
  112.6 2.2 %copy.14 = f32[64,3584]{1,0:T(8,128)} copy(f32[64,3584]{1,0:T(8,128)} %get-tuple-element.9) | data formatting | bytes 1835008
  114.8 0.0 copy-done.6
  114.8 0.0 copy-start.5
  114.8 0.9 copy.15
  115.8 0.6 copy-done.5
  116.4 0.9 copy.16
Async XLA Ops:
  0.6 1.0 copy-start
  1.7 1.0 copy-start.1
  2.7 1.0 copy-start.2
  3.7 0.8 copy-start.3
  4.4 0.8 copy-start.4
  112.6 2.3 %copy-start.6 = (f32[64,3584]{1,0:T(8,128)S(1)}, f32[64,3584]{1,0:T(8,128)}, u32[]{:S(2)}) copy-start(f32[64,3584]{1,0:T(8,128)} %get-tuple-element.10) | copy-start | bytes 2752516
  114.8 1.5 %copy-start.5 = (f32[448,512]{1,0:T(8,128)S(1)}, f32[448,512]{1,0:T(8,128)}, u32[]{:S(2)}) copy-start(f32[448,512]{1,0:T(8,128)} %get-tuple-element.11) | copy-start | bytes 2752516

commit v3 on v2

v3 whole, which is shorter than its diff:
```python
import jax
import jax.numpy as jnp
from jax import lax
from jax.experimental import pallas as pl
from jax.experimental.pallas import tpu as pltpu
from jax.sharding import PartitionSpec as P

F32, BF16 = jnp.float32, jnp.bfloat16
MESH = pl.DeviceIdType.MESH
NX, NY, NZH = 4, 4, 4
SUB = 112
HALF = 512
COPIES = 160


def nt(left_side, right_side):
    return lax.dot_general(left_side, right_side, (((1,), (1,)), ((), ())), preferred_element_type=F32)


def nn(left_side, right_side):
    return jnp.dot(left_side, right_side, preferred_element_type=F32)


def tn(left_side, right_side):
    return lax.dot_general(left_side, right_side, (((0,), (0,)), ((), ())), preferred_element_type=F32)


def local_step(gate_value, up_value, hidden_grad):
    logistic = 1.0 / (1.0 + jnp.exp(-gate_value))
    activated = gate_value * logistic
    hidden = (activated * up_value).astype(BF16)
    up_grad = (hidden_grad * activated).astype(BF16)
    gate_grad = (hidden_grad * up_value * logistic * (1.0 + gate_value * (1.0 - logistic))).astype(BF16)
    return (hidden, gate_grad, up_grad)


def lanes(block):
    return pl.ds(pl.multiple_of(block * 128, 128), 128)


def kernel(
    tok_hbm, cot_hbm, gate_hbm, up_hbm, down_hbm,
    tg_out, wg_out, down_out,
    tok_in, cot_in, gate_in, up_in, down_in,
    wt, wblk, gu, tok, cot, rs_send, rs_recv, hg_send, hg_recv, hg_own, pair,
    grads, hid, wg_send, wg_recv, part, ta_send, ta_recv, tb_send, tb_recv, tc_send, tc_recv,
    load_sems, send_sems, recv_sems,
):
    inp, y, dep = lax.axis_index("inp"), lax.axis_index("out"), lax.axis_index("dep")
    zl, x = inp // NX, inp % NX
    zh, c = dep // 2, dep % 2
    z = zh * 2 + zl

    def at(x_=x, y_=y, zh_=zh, zl_=zl, c_=c):
        return (zl_ * NX + x_, y_, zh_ * 2 + c_)

    def ring(step):
        there = (z + step + 8) % 8
        return (there // 2, there % 2)

    xs = [(x + k) % NX for k in range(NX)]
    ys = [(y + k) % NY for k in range(NY)]
    zhs = [(zh + k) % NZH for k in range(NZH)]
    cs = [c, 1 - c]
    sides = [ring(1), ring(-1)]
    around = [at(zh_=side[0], zl_=side[1]) for side in sides]
    partner = at(zl_=1 - zl)

    loads = []
    for src, dst in (
        (gate_hbm, gate_in), (up_hbm, up_in), (tok_hbm, tok_in), (cot_hbm, cot_in), (down_hbm, down_in)
    ):
        loads.append(pltpu.make_async_copy(src, dst, load_sems.at[len(loads)]))
        loads[-1].start()

    peers = [at(zh_=zhs[m], y_=ys[k]) for m in range(1, NZH) for k in range(NY)]
    peers += [at(x_=xs[k], zh_=zhs[m]) for m in range(1, NZH) for k in range(1, NX)]
    peers += around
    peers += [at(y_=ys[k]) for k in range(1, NY)]
    peers += [at(x_=xs[k], c_=cs[e]) for k in range(1, NX) for e in range(2)]
    peers += [at(c_=cs[1])]
    barrier = pltpu.get_barrier_semaphore()
    for peer in peers:
        pl.semaphore_signal(barrier, inc=1, device_id=peer, device_id_type=MESH)

    for load in loads:
        load.wait()

    for q in range(NZH):
        columns = pl.ds(q * 896, 896)
        both = jnp.concatenate((gate_in[:, columns], up_in[:, columns]), axis=0)
        wt[q] = both.T.reshape(2, NX, SUB, 128)
    wblk[x * 2 + c] = wt[:, c, x]
    tok[zh, c, y, :, lanes(x)] = tok_in[:, lanes(zh)]
    cot[zh, c, y] = cot_in[...]

    pl.semaphore_wait(barrier, len(peers))

    started = []

    def send(src, dst, device):
        index = len(started)
        copy = pltpu.make_async_remote_copy(
            src_ref=src, dst_ref=dst, send_sem=send_sems.at[index], recv_sem=recv_sems.at[index],
            device_id=device, device_id_type=MESH,
        )
        copy.start()
        started.append(copy)
        return copy

    def arrive(copies):
        for copy in copies:
            copy.wait_recv()

    tok_first = [
        send(tok_in.at[:, lanes(zhs[m])], tok.at[zh, c, y, :, lanes(x)], at(x_=xs[k], zh_=zhs[m]))
        for m in (2, 1, 3, 0) for k in (2, 1, 3, 0) if (m, k) != (0, 0)
    ]
    cot_first = [send(cot_in, cot.at[zh, c, y], at(zh_=zhs[m])) for m in (2, 1, 3)]

    def send_weights(q):
        return [
            send(wt.at[q, cs[e], xs[k]], wblk.at[x * 2 + c, q], at(x_=xs[k], c_=cs[e]))
            for k in (2, 1, 3, 0) for e in range(2) if (k, e) != (0, 0)
        ]

    def spread(buffer, first):
        arrive(first)
        own = buffer.at[:, c, y]
        return {k: send(own, own, at(y_=ys[k])) for k in (2, 1, 3)}, [send(own, own, at(c_=cs[1]))]

    def share(buffer, by_y, by_core):
        for k in (1, 3, 2):
            by_y[k].wait_recv()
            rows = buffer.at[:, c, ys[NY - k]]
            by_core.append(send(rows, rows, at(c_=cs[1])))

    order = [zhs[2], zhs[1], zhs[3], zhs[0]]
    weights = [send_weights(order[0])]
    tok_y, tok_core = spread(tok, tok_first)
    cot_y, cot_core = spread(cot, cot_first)
    for q in range(1, NZH):
        weights.append(send_weights(order[q]))

    def assemble(q):
        arrive(weights[q])
        for k in range(NX):
            even, odd = wblk[2 * k, order[q]], wblk[2 * k + 1, order[q]]
            here = pl.ds(k * 128, 128)
            gu[0, order[q], :, here] = jnp.concatenate((even[:, :64], odd[:, :64]), axis=1)
            gu[1, order[q], :, here] = jnp.concatenate((even[:, 64:], odd[:, 64:]), axis=1)

    assemble(0)
    share(tok, tok_y, tok_core)
    arrive(tok_core)

    def partial(there):
        rows = gu[:, there[0]].reshape(2 * SUB, HALF)
        seen = tok[pl.ds(there[1] * 2, 2)].reshape(HALF, HALF)
        return nt(rows, seen).reshape(2, SUB, HALF)

    halves = [pl.ds(0, 256), pl.ds(256, 256)]
    own = partial(ring(4)).astype(BF16)
    rs_send[0, 0] = own
    rs_send[1, 0] = own
    moving = [
        [send(rs_send.at[d, 0, m, :, halves[d]], rs_recv.at[d, 0, m, :, halves[d]], around[d]) for d in range(2)]
        for m in range(2)
    ]
    assemble(1)
    assemble(2)

    share(cot, cot_y, cot_core)
    arrive(cot_core)

    def hidden_part(q):
        rows = down_in[pl.ds(pl.multiple_of(q * SUB, 16), SUB), :]
        return nt(rows, cot[...].reshape(2 * HALF, HALF))

    by_x = []
    for k in (2, 1, 3):
        some = hidden_part(xs[k]).astype(BF16)
        hg_send[k - 1, 0] = some[:, :HALF]
        hg_send[k - 1, 1] = some[:, HALF:]
        by_x.append(send(hg_send.at[k - 1], hg_recv.at[k - 1], at(x_=xs[k])))

    def onward(step, moving):
        terms = [partial(ring(4 - step)), partial(ring(step - 4))]
        later = []
        for m in range(2):
            row = []
            for d in range(2):
                moving[m][d].wait_recv()
                if step == 1:
                    came = rs_recv[d, 0, m, :, halves[d]].astype(F32)
                    sides = [terms[d][m][:, :256], terms[d][m][:, 256:]]
                    sides[d] = sides[d] + came
                    total = jnp.concatenate(sides, axis=1)
                else:
                    total = terms[d][m] + rs_recv[d, step - 1, m].astype(F32)
                rs_send[d, step, m] = total.astype(BF16)
                row.append(send(rs_send.at[d, step, m], rs_recv.at[d, step, m], around[d]))
            later.append(row)
        return later

    moving = onward(1, moving)
    assemble(3)
    some = hidden_part(x)
    hg_own[0] = some[:, :HALF]
    hg_own[1] = some[:, HALF:]
    moving = onward(2, moving)

    def hidden_sum(half):
        total = hg_own[half]
        for k in range(NX - 1):
            total = total + hg_recv[k, half].astype(F32)
        return total

    arrive(by_x)
    pair[0] = hidden_sum(1 - zl).astype(BF16)
    by_pair = send(pair.at[0], pair.at[1], partner)
    moving = onward(3, moving)
    hidden_grad = hidden_sum(zl)
    values = partial((zh, zl))
    by_pair.wait_recv()
    hidden_grad = hidden_grad + pair[1].astype(F32)
    sums = []
    for m in range(2):
        total = values[m]
        for d in range(2):
            moving[m][d].wait_recv()
            total = total + rs_recv[d, 3, m].astype(F32)
        sums.append(total)
    hidden, gate_grad, up_grad = local_step(sums[0], sums[1], hidden_grad)

    grads[zl, 0, zh] = gate_grad
    grads[zl, 1, zh] = up_grad

    def chunk(there, m, step, d):
        if step == 3:
            return grads.at[there[1], m, there[0], :, halves[d]]
        return grads.at[there[1], m, there[0]]

    def forward(step, m):
        row = []
        for d in range(2):
            block = chunk(ring(-step if d == 0 else step), m, step, d)
            row.append(send(block, block, around[d]))
        return row

    moving = [forward(0, m) for m in range(2)]
    hid[zl, x] = hidden
    by_pair = send(hid.at[zl, x], hid.at[zl, x], partner)

    returned = []

    def weight_grads(q):
        both = nn(grads[0, :, q].reshape(2 * SUB, HALF), tok[0:2].reshape(HALF, HALF))
        both = both + nn(grads[1, :, q].reshape(2 * SUB, HALF), tok[2:4].reshape(HALF, HALF))
        both = both.astype(BF16)
        for k in range(NX):
            here = both[:, k * 128 : (k + 1) * 128]
            wg_send[q, 0, k] = jnp.concatenate((here[:SUB, :64], here[SUB:, :64]), axis=1)
            wg_send[q, 1, k] = jnp.concatenate((here[:SUB, 64:], here[SUB:, 64:]), axis=1)
        wg_recv[q, c, x] = wg_send[q, c, x]
        for k in (2, 1, 3, 0):
            for e in range(2):
                if (k, e) != (0, 0):
                    returned.append(
                        send(wg_send.at[q, cs[e], xs[k]], wg_recv.at[q, c, x], at(x_=xs[k], c_=cs[e]))
                    )

    def over_core(p, half):
        term = tn(grads[half].reshape(8 * SUB, HALF), gu[...].reshape(8 * SUB, HALF))
        part[p] = term.reshape(2, 2, NY, 32, HALF)
        ta_send[p] = part[p, :, cs[1]].astype(BF16)
        return send(ta_send.at[p], ta_recv.at[p], at(c_=cs[1]))

    def over_x(p, by_core):
        by_core.wait_recv()
        total = part[p, :, c] + ta_recv[p].astype(F32)
        part[p, :, c] = total
        for k in range(NX):
            tb_send[p, k] = total[:, :, :, k * 128 : (k + 1) * 128].astype(BF16)
        return [send(tb_send.at[p, xs[k]], tb_recv.at[p, k - 1], at(x_=xs[k])) for k in (2, 1, 3)]

    def sum_x(p, half, by_x):
        arrive(by_x)
        total = part[p, :, c, :, :, lanes(x)]
        for k in range(NX - 1):
            total = total + tb_recv[p, k].astype(F32)
        tc_send[pl.ds(half * 2, 2)] = total.astype(BF16)

    turn = 2 * zl - 1
    finished = [zh, (zh + turn + NZH) % NZH, (zh - turn + NZH) % NZH, zhs[2]]
    for step in range(4):
        later = []
        for m in range(2):
            arrive(moving[m])
            if step < 3:
                later.append(forward(step + 1, m))
        moving = later
        if step == 0:
            by_pair.wait_recv()
            by_x = [send(hid.at[:, x], hid.at[:, x], at(x_=xs[k])) for k in (2, 1, 3)]
        if step == 2:
            early = over_x(0, over_core(0, 1 - zl))
        if step < 2:
            weight_grads(finished[step])
    by_core = over_core(1, zl)
    sum_x(0, 1 - zl, early)
    late = over_x(1, by_core)
    weight_grads(finished[2])
    weight_grads(finished[3])
    sum_x(1, zl, late)
    by_place = [
        send(tc_send.at[zhs[m], ys[k]], tc_recv.at[zh, k], at(zh_=zhs[m], y_=ys[k]))
        for m in (2, 1, 3, 0) for k in (2, 1, 3, 0) if (m, k) != (0, 0)
    ]
    tc_recv[zh, 0] = tc_send[zh, y]
    arrive(by_x)
    down_out[...] = nn(hid[0].reshape(4 * SUB, HALF), cot[0:2].reshape(HALF, HALF)) + nn(
        hid[1].reshape(4 * SUB, HALF), cot[2:4].reshape(HALF, HALF)
    )
    arrive(returned)
    wg_out[...] = wg_recv[...].reshape(NZH, 896, 128)
    arrive(by_place)
    for q in range(NZH):
        total = tc_recv[q, 0].astype(F32)
        for k in range(1, NY):
            total = total + tc_recv[q, k].astype(F32)
        tg_out[:, pl.ds(q * 128, 128)] = total
    for copy in started:
        copy.wait_send()


def finish(tg_in, wg_in, down_in, tg_out, gate_out, up_out, down_out):
    for q in range(NZH):
        block = wg_in[q].T.astype(F32)
        gate_out[:, pl.ds(q * 896, 896)] = block[:64]
        up_out[:, pl.ds(q * 896, 896)] = block[64:]
    down_out[...] = down_in[...]
    tg_out[...] = tg_in[...]


def shards(tokens, cotangent, gate_weight, up_weight, down_weight):
    vmem = pl.BlockSpec(memory_space=pltpu.VMEM)
    hbm = pl.BlockSpec(memory_space=pltpu.HBM)
    outs = [
        jax.ShapeDtypeStruct(tokens.shape, F32),
        jax.ShapeDtypeStruct(gate_weight.shape, F32),
        jax.ShapeDtypeStruct(up_weight.shape, F32),
        jax.ShapeDtypeStruct(down_weight.shape, F32),
    ]
    between = [
        outs[0],
        jax.ShapeDtypeStruct((NZH, 896, 128), BF16),
        outs[3],
    ]
    scratch = [
        pltpu.VMEM(tokens.shape, BF16),
        pltpu.VMEM(cotangent.shape, BF16),
        pltpu.VMEM(gate_weight.shape, BF16),
        pltpu.VMEM(up_weight.shape, BF16),
        pltpu.VMEM(down_weight.shape, BF16),
        pltpu.VMEM((NZH, 2, NX, SUB, 128), BF16),
        pltpu.VMEM((2 * NX, NZH, SUB, 128), BF16),
        pltpu.VMEM((2, NZH, SUB, HALF), BF16),
        pltpu.VMEM((NZH, 2, NY, 32, HALF), BF16),
        pltpu.VMEM((NZH, 2, NY, 32, HALF), BF16),
        pltpu.VMEM((2, 4, 2, SUB, HALF), BF16),
        pltpu.VMEM((2, 4, 2, SUB, HALF), BF16),
        pltpu.VMEM((NX - 1, 2, SUB, HALF), BF16),
        pltpu.VMEM((NX - 1, 2, SUB, HALF), BF16),
        pltpu.VMEM((2, SUB, HALF), F32),
        pltpu.VMEM((2, SUB, HALF), BF16),
        pltpu.VMEM((2, 2, NZH, SUB, HALF), BF16),
        pltpu.VMEM((2, NX, SUB, HALF), BF16),
        pltpu.VMEM((NZH, 2, NX, SUB, 128), BF16),
        pltpu.VMEM((NZH, 2, NX, SUB, 128), BF16),
        pltpu.VMEM((2, 2, 2, NY, 32, HALF), F32),
        pltpu.VMEM((2, 2, NY, 32, HALF), BF16),
        pltpu.VMEM((2, 2, NY, 32, HALF), BF16),
        pltpu.VMEM((2, NX, 2, NY, 32, 128), BF16),
        pltpu.VMEM((2, NX - 1, 2, NY, 32, 128), BF16),
        pltpu.VMEM((NZH, NY, 32, 128), BF16),
        pltpu.VMEM((NZH, NY, 32, 128), BF16),
        pltpu.SemaphoreType.DMA((5,)),
        pltpu.SemaphoreType.DMA((COPIES,)),
        pltpu.SemaphoreType.DMA((COPIES,)),
    ]
    token_grad, weight_grad, down_grad = pl.pallas_call(
        kernel,
        out_shape=between,
        in_specs=[hbm] * 5,
        out_specs=[vmem] * 3,
        scratch_shapes=scratch,
        compiler_params=pltpu.CompilerParams(
            collective_id=0, has_side_effects=True, vmem_limit_bytes=60 * 2**20
        ),
        name="layer",
    )(tokens, cotangent, gate_weight, up_weight, down_weight)
    return pl.pallas_call(
        finish,
        out_shape=outs,
        in_specs=[vmem] * 3,
        out_specs=[vmem] * 4,
        compiler_params=pltpu.CompilerParams(vmem_limit_bytes=60 * 2**20),
        name="finish",
    )(token_grad, weight_grad, down_grad)


def solution(mesh):
    return jax.shard_map(
        shards,
        mesh=mesh,
        in_specs=(
            P(("dep", "out"), "inp"),
            P(("dep", "out"), "inp"),
            P(("inp", "dep"), "out"),
            P(("inp", "dep"), "out"),
            P(("out", "dep"), "inp"),
        ),
        out_specs=(
            P(("dep", "out"), "inp"),
            P(("inp", "dep"), "out"),
            P(("inp", "dep"), "out"),
            P(("out", "dep"), "inp"),
        ),
        check_vma=False,
    )
```

time: 118 us -> 102 us (0.86)
  local copies, waits for them, and re-layouts: 9.88 us -> 0 us
  Pallas kernels: 107 us -> 101 us
    unnamed x18 -> x0, local copies, waits for them, and re-layouts: 9.88 us -> none
    pallas_call x1 -> x2, Pallas kernels: 107 us -> 101 us  [the longest x1 97.6 us: shards(): pl.pallas_call(kernel, out_shape=between, in_specs=[hbm] * 5, out_specs=[...]
where the time goes in v3:
time: 102 us
  Pallas kernels  101 us (99%)
    pallas_call x1, Pallas kernels, shards(): pl.pallas_call(kernel, out_shape=between, in_specs=[hbm] * 5, out_specs=[...  97.6 us
    pallas_call x1, Pallas kernels, shards(): pl.pallas_call(finish, out_shape=outs, in_specs=[vmem] * 3, out_specs=[vm...  3.31 us

profile of v3, /device:TPU:1, one launch (start us, length us, event | category | flops | bytes accessed | tf_op | source)
XLA Modules:
  0.0 101.6 jit_solution(12360836237820078361)
XLA Ops:
  0.6 97.6 %layer.1 = (f32[32,512]{1,0:T(8,128)}, bf16[4,896,128]{2,1,0:T(8,128)(2,1)}, f32[448,512]{1,0:T(8,128)}) custom-call(bf16[32,512]{1,0:T(8,128)(2,1)} %tok_hbm.1, bf16[32,512]{1,0:T(8,128)(2,1)} %cot_hbm.1, bf16[64,3584]{1,0:T(8,128)(2,1)} %gate_hbm.1, bf16[64,3584]{1,0:T(8,128)(2,1)} %up_hbm.1, bf16[448,512]{1,0:T(8,128)(2,1)} %down_hbm.1), custom_call_target="tpu_custom_call" | custom-call | tf_op jit(solution)/shard_map/layer/pallas_call | solution.py:392
  98.3 3.3 %finish.1 = (f32[32,512]{1,0:T(8,128)}, f32[64,3584]{1,0:T(8,128)}, f32[64,3584]{1,0:T(8,128)}, f32[448,512]{1,0:T(8,128)}) custom-call(f32[32,512]{1,0:T(8,128)} %get-tuple-element.7.tg_in, bf16[4,896,128]{2,1,0:T(8,128)(2,1)} %get-tuple-element.8.wg_in, f32[448,512]{1,0:T(8,128)} %get-tuple-element.9.down_in), custom_call_target="tpu_custom_call" | custom-call | tf_op jit(solution)/shard_map/finish/pallas_call | solution.py:403

commit v4 on v3

v4 whole, which is shorter than its diff:
```python
import jax
import jax.numpy as jnp
from jax import lax
from jax.experimental import pallas as pl
from jax.experimental.pallas import tpu as pltpu
from jax.sharding import PartitionSpec as P

F32, BF16 = jnp.float32, jnp.bfloat16
MESH = pl.DeviceIdType.MESH
NX, NY, NZH = 4, 4, 4
SUB = 112
HALF = 512
PHASE = 256
COPIES = 180


def nt(left_side, right_side):
    return lax.dot_general(left_side, right_side, (((1,), (1,)), ((), ())), preferred_element_type=F32)


def nn(left_side, right_side):
    return jnp.dot(left_side, right_side, preferred_element_type=F32)


def tn(left_side, right_side):
    return lax.dot_general(left_side, right_side, (((0,), (0,)), ((), ())), preferred_element_type=F32)


def local_step(gate_value, up_value, hidden_grad):
    logistic = 1.0 / (1.0 + jnp.exp(-gate_value))
    activated = gate_value * logistic
    hidden = (activated * up_value).astype(BF16)
    up_grad = (hidden_grad * activated).astype(BF16)
    gate_grad = (hidden_grad * up_value * logistic * (1.0 + gate_value * (1.0 - logistic))).astype(BF16)
    return (hidden, gate_grad, up_grad)


def lanes(block):
    return pl.ds(pl.multiple_of(block * 128, 128), 128)


def kernel(
    tok_hbm, cot_hbm, gate_hbm, up_hbm, down_hbm,
    tg_out, wg_out, down_out,
    tok_in, cot_in, gate_in, up_in, down_in,
    wt, wblk, gu, tok, cot, rs_send, rs_recv, hg_send, hg_recv, hg_own, pair,
    grads, hid, wg_send, wg_recv, part, ta_send, ta_recv, tb_send, tb_recv, tc_send, tc_recv,
    load_sems, send_sems, recv_sems,
):
    inp, y, dep = lax.axis_index("inp"), lax.axis_index("out"), lax.axis_index("dep")
    zl, x = inp // NX, inp % NX
    zh, c = dep // 2, dep % 2
    z = zh * 2 + zl

    def at(x_=x, y_=y, zh_=zh, zl_=zl, c_=c):
        return (zl_ * NX + x_, y_, zh_ * 2 + c_)

    def ring(step):
        there = (z + step + 8) % 8
        return (there // 2, there % 2)

    xs = [(x + k) % NX for k in range(NX)]
    ys = [(y + k) % NY for k in range(NY)]
    zhs = [(zh + k) % NZH for k in range(NZH)]
    cs = [c, 1 - c]
    sides = [ring(1), ring(-1)]
    around = [at(zh_=side[0], zl_=side[1]) for side in sides]
    partner = at(zl_=1 - zl)

    loads = []
    for src, dst in (
        (gate_hbm, gate_in), (up_hbm, up_in), (tok_hbm, tok_in), (cot_hbm, cot_in), (down_hbm, down_in)
    ):
        loads.append(pltpu.make_async_copy(src, dst, load_sems.at[len(loads)]))
        loads[-1].start()

    peers = [at(zh_=zhs[m], y_=ys[k]) for m in range(1, NZH) for k in range(NY)]
    peers += [at(x_=xs[k], zh_=zhs[m]) for m in range(1, NZH) for k in range(1, NX)]
    peers += around
    peers += [at(y_=ys[k]) for k in range(1, NY)]
    peers += [at(x_=xs[k], c_=cs[e]) for k in range(1, NX) for e in range(2)]
    peers += [at(c_=cs[1])]
    barrier = pltpu.get_barrier_semaphore()
    for peer in peers:
        pl.semaphore_signal(barrier, inc=1, device_id=peer, device_id_type=MESH)

    for load in loads:
        load.wait()

    for q in range(NZH):
        columns = pl.ds(q * 896, 896)
        both = jnp.concatenate((gate_in[:, columns], up_in[:, columns]), axis=0)
        wt[q] = both.T.reshape(2, NX, SUB, 128)
    wblk[x * 2 + c] = wt[:, c, x]
    tok[zh // 2, zh % 2, c, y, :, lanes(x)] = tok_in[:, lanes(zh)]
    cot[zh // 2, zh % 2, c, y] = cot_in[...]

    pl.semaphore_wait(barrier, len(peers))

    started = []

    def send(src, dst, device):
        index = len(started)
        copy = pltpu.make_async_remote_copy(
            src_ref=src, dst_ref=dst, send_sem=send_sems.at[index], recv_sem=recv_sems.at[index],
            device_id=device, device_id_type=MESH,
        )
        copy.start()
        started.append(copy)
        return copy

    def arrive(copies):
        for copy in copies:
            copy.wait_recv()

    tok_first = [
        send(
            tok_in.at[:, lanes(zhs[m])],
            tok.at[zh // 2, zh % 2, c, y, :, lanes(x)],
            at(x_=xs[k], zh_=zhs[m]),
        )
        for m in (2, 1, 3, 0) for k in (2, 1, 3, 0) if (m, k) != (0, 0)
    ]
    cot_first = [send(cot_in, cot.at[zh // 2, zh % 2, c, y], at(zh_=zhs[m])) for m in (2, 1, 3)]

    def send_weights(q):
        return [
            send(wt.at[q, cs[e], xs[k]], wblk.at[x * 2 + c, q], at(x_=xs[k], c_=cs[e]))
            for k in (2, 1, 3, 0) for e in range(2) if (k, e) != (0, 0)
        ]

    def spread(buffer, p):
        own = buffer.at[:, p, c, y]
        return {k: send(own, own, at(y_=ys[k])) for k in (2, 1, 3)}, [send(own, own, at(c_=cs[1]))]

    def share(buffer, p, by_y, by_core):
        for k in (1, 3, 2):
            by_y[k].wait_recv()
            rows = buffer.at[:, p, c, ys[NY - k]]
            by_core.append(send(rows, rows, at(c_=cs[1])))
        arrive(by_core)

    order = [zhs[2], zhs[1], zhs[3], zhs[0]]
    weights = [send_weights(order[0])]
    arrive(tok_first)
    tok_later = [spread(tok, p) for p in range(2)]
    arrive(cot_first)
    cot_later = [spread(cot, p) for p in range(2)]
    for q in range(1, NZH):
        weights.append(send_weights(order[q]))

    def assemble(q):
        arrive(weights[q])
        for k in range(NX):
            even, odd = wblk[2 * k, order[q]], wblk[2 * k + 1, order[q]]
            here = pl.ds(k * 128, 128)
            gu[0, order[q], :, here] = jnp.concatenate((even[:, :64], odd[:, :64]), axis=1)
            gu[1, order[q], :, here] = jnp.concatenate((even[:, 64:], odd[:, 64:]), axis=1)

    def partial(there, p):
        rows = gu[:, there[0]].reshape(2 * SUB, HALF)
        return nt(rows, tok[there[1], p].reshape(PHASE, HALF)).reshape(2, SUB, PHASE)

    halves = [pl.ds(0, 128), pl.ds(128, 128)]

    def outset(p):
        own = partial(ring(4), p).astype(BF16)
        row = []
        for d in range(2):
            rs_send[p, d, 0, :, :, halves[d]] = own[:, :, d * 128 : (d + 1) * 128]
            row.append(
                send(rs_send.at[p, d, 0, :, :, halves[d]], rs_recv.at[p, d, 0, :, :, halves[d]], around[d])
            )
        return row

    def onward(step, p, row):
        terms = [partial(ring(4 - step), p), partial(ring(step - 4), p)]
        later = []
        for d in range(2):
            row[d].wait_recv()
            if step == 1:
                came = rs_recv[p, d, 0, :, :, halves[d]].astype(F32)
                two = [terms[d][:, :, :128], terms[d][:, :, 128:]]
                two[d] = two[d] + came
                total = jnp.concatenate(two, axis=2)
            else:
                total = terms[d] + rs_recv[p, d, step - 1].astype(F32)
            rs_send[p, d, step] = total.astype(BF16)
            later.append(send(rs_send.at[p, d, step], rs_recv.at[p, d, step], around[d]))
        return later

    def hidden_part(q, p):
        rows = down_in[pl.ds(pl.multiple_of(q * SUB, 16), SUB), :]
        return nt(rows, cot[:, p].reshape(2 * PHASE, HALF))

    def hidden_over_x(p):
        share(cot, p, *cot_later[p])
        copies = []
        for k in (2, 1, 3):
            some = hidden_part(xs[k], p).astype(BF16)
            for half in range(2):
                hg_send[p, k - 1, half] = some[:, half * PHASE : (half + 1) * PHASE]
            copies.append(send(hg_send.at[p, k - 1], hg_recv.at[p, k - 1], at(x_=xs[k])))
        some = hidden_part(x, p)
        for half in range(2):
            hg_own[p, half] = some[:, half * PHASE : (half + 1) * PHASE]
        return copies

    def hidden_sum(p, half):
        total = hg_own[p, half]
        for k in range(NX - 1):
            total = total + hg_recv[p, k, half].astype(F32)
        return total

    def hidden_pair(p, by_x):
        arrive(by_x)
        pair[p, 0] = hidden_sum(p, 1 - zl).astype(BF16)
        return send(pair.at[p, 0], pair.at[p, 1], partner)

    assemble(0)
    moving, by_x, by_pair = [None, None], [None, None], [None, None]
    for p in range(2):
        share(tok, p, *tok_later[p])
        moving[p] = outset(p)
    assemble(1)
    assemble(2)
    for p in range(2):
        moving[p] = onward(1, p, moving[p])
        by_x[p] = hidden_over_x(p)
    assemble(3)
    for p in range(2):
        moving[p] = onward(2, p, moving[p])
    by_pair[0] = hidden_pair(0, by_x[0])
    for p in range(2):
        moving[p] = onward(3, p, moving[p])
    by_pair[1] = hidden_pair(1, by_x[1])

    def chunk(there, p, step, d):
        if step == 3:
            return grads.at[there[1], p, :, there[0], :, halves[d]]
        return grads.at[there[1], p, :, there[0]]

    def forward(step, p):
        row = []
        for d in range(2):
            block = chunk(ring(-step if d == 0 else step), p, step, d)
            row.append(send(block, block, around[d]))
        return row

    for p in range(2):
        values = partial((zh, zl), p)
        hidden_grad = hidden_sum(p, zl)
        by_pair[p].wait_recv()
        hidden_grad = hidden_grad + pair[p, 1].astype(F32)
        for d in range(2):
            moving[p][d].wait_recv()
            values = values + rs_recv[p, d, 3].astype(F32)
        hidden, gate_grad, up_grad = local_step(values[0], values[1], hidden_grad)
        grads[zl, p, 0, zh] = gate_grad
        grads[zl, p, 1, zh] = up_grad
        moving[p] = forward(0, p)
        hid[zl, p, x] = hidden
        by_pair[p] = send(hid.at[zl, p, x], hid.at[zl, p, x], partner)

    returned = []

    def weight_grads(q):
        both = jnp.zeros((2 * SUB, HALF), F32)
        for half in range(2):
            for p in range(2):
                rows = grads[half, p, :, q].reshape(2 * SUB, PHASE)
                both = both + nn(rows, tok[half, p].reshape(PHASE, HALF))
        both = both.astype(BF16)
        for k in range(NX):
            here = both[:, k * 128 : (k + 1) * 128]
            wg_send[q, 0, k] = jnp.concatenate((here[:SUB, :64], here[SUB:, :64]), axis=1)
            wg_send[q, 1, k] = jnp.concatenate((here[:SUB, 64:], here[SUB:, 64:]), axis=1)
        wg_recv[q, c, x] = wg_send[q, c, x]
        for k in (2, 1, 3, 0):
            for e in range(2):
                if (k, e) != (0, 0):
                    returned.append(
                        send(wg_send.at[q, cs[e], xs[k]], wg_recv.at[q, c, x], at(x_=xs[k], c_=cs[e]))
                    )

    def over_core(p):
        for half in range(2):
            term = tn(grads[half, p].reshape(8 * SUB, PHASE), gu[...].reshape(8 * SUB, HALF))
            part[p, half] = term.reshape(2, NY, 32, HALF)
        ta_send[p] = part[p, :, cs[1]].astype(BF16)
        return send(ta_send.at[p], ta_recv.at[p], at(c_=cs[1]))

    def over_x(p, by_core):
        by_core.wait_recv()
        total = part[p, :, c] + ta_recv[p].astype(F32)
        part[p, :, c] = total
        for k in range(NX):
            tb_send[p, k] = total[:, :, :, k * 128 : (k + 1) * 128].astype(BF16)
        return [send(tb_send.at[p, xs[k]], tb_recv.at[p, k - 1], at(x_=xs[k])) for k in (2, 1, 3)]

    def sum_x(p, by_x):
        arrive(by_x)
        total = part[p, :, c, :, :, lanes(x)]
        for k in range(NX - 1):
            total = total + tb_recv[p, k].astype(F32)
        tc_send[:, p] = total.astype(BF16)

    turn = 2 * zl - 1
    finished = [zh, (zh + turn + NZH) % NZH, (zh - turn + NZH) % NZH, zhs[2]]
    for step in range(3):
        for p in range(2):
            arrive(moving[p])
            moving[p] = forward(step + 1, p)
            if step == 0:
                by_pair[p].wait_recv()
                by_x[p] = [send(hid.at[:, p, x], hid.at[:, p, x], at(x_=xs[k])) for k in (2, 1, 3)]
        if step < 2:
            weight_grads(finished[step])
    arrive(moving[0])
    early = over_x(0, over_core(0))
    arrive(moving[1])
    late = over_x(1, over_core(1))
    weight_grads(finished[2])
    weight_grads(finished[3])
    sum_x(0, early)
    sum_x(1, late)
    by_place = [
        send(
            tc_send.at[zhs[m] // 2, zhs[m] % 2, ys[k]], tc_recv.at[zh, k], at(zh_=zhs[m], y_=ys[k])
        )
        for m in (2, 1, 3, 0) for k in (2, 1, 3, 0) if (m, k) != (0, 0)
    ]
    tc_recv[zh, 0] = tc_send[zh // 2, zh % 2, y]
    arrive(by_x[0])
    arrive(by_x[1])
    down = jnp.zeros((4 * SUB, HALF), F32)
    for half in range(2):
        for p in range(2):
            rows = hid[half, p].reshape(4 * SUB, PHASE)
            down = down + nn(rows, cot[half, p].reshape(PHASE, HALF))
    down_out[...] = down
    arrive(returned)
    wg_out[...] = wg_recv[...].reshape(NZH, 896, 128)
    arrive(by_place)
    for q in range(NZH):
        total = tc_recv[q, 0].astype(F32)
        for k in range(1, NY):
            total = total + tc_recv[q, k].astype(F32)
        tg_out[:, pl.ds(q * 128, 128)] = total
    for copy in started:
        copy.wait_send()


def finish(tg_in, wg_in, down_in, tg_out, gate_out, up_out, down_out, tg, wg, down, gate, up, sems):
    loads = [pltpu.make_async_copy(wg_in.at[q], wg.at[q], sems.at[q]) for q in range(NZH)]
    loads.append(pltpu.make_async_copy(down_in, down, sems.at[NZH]))
    loads.append(pltpu.make_async_copy(tg_in, tg, sems.at[NZH + 1]))
    for load in loads:
        load.start()
    stores = []

    def store(src, dst):
        stores.append(pltpu.make_async_copy(src, dst, sems.at[len(loads) + len(stores)]))
        stores[-1].start()

    for q in range(NZH):
        loads[q].wait()
        here = pl.ds(q * 896, 896)
        block = wg[q].T.astype(F32)
        for rows, buffer, out in ((block[:64], gate, gate_out), (block[64:], up, up_out)):
            buffer[:, here] = rows
            store(buffer.at[:, here], out.at[:, here])
        if q == 1:
            loads[NZH].wait()
            store(down, down_out)
            loads[NZH + 1].wait()
            store(tg, tg_out)
    for copy in stores:
        copy.wait()


def shards(tokens, cotangent, gate_weight, up_weight, down_weight):
    vmem = pl.BlockSpec(memory_space=pltpu.VMEM)
    hbm = pl.BlockSpec(memory_space=pltpu.HBM)
    outs = [
        jax.ShapeDtypeStruct(tokens.shape, F32),
        jax.ShapeDtypeStruct(gate_weight.shape, F32),
        jax.ShapeDtypeStruct(up_weight.shape, F32),
        jax.ShapeDtypeStruct(down_weight.shape, F32),
    ]
    between = [
        outs[0],
        jax.ShapeDtypeStruct((NZH, 896, 128), BF16),
        outs[3],
    ]
    scratch = [
        pltpu.VMEM(tokens.shape, BF16),
        pltpu.VMEM(cotangent.shape, BF16),
        pltpu.VMEM(gate_weight.shape, BF16),
        pltpu.VMEM(up_weight.shape, BF16),
        pltpu.VMEM(down_weight.shape, BF16),
        pltpu.VMEM((NZH, 2, NX, SUB, 128), BF16),
        pltpu.VMEM((2 * NX, NZH, SUB, 128), BF16),
        pltpu.VMEM((2, NZH, SUB, HALF), BF16),
        pltpu.VMEM((2, 2, 2, NY, 32, HALF), BF16),
        pltpu.VMEM((2, 2, 2, NY, 32, HALF), BF16),
        pltpu.VMEM((2, 2, 4, 2, SUB, PHASE), BF16),
        pltpu.VMEM((2, 2, 4, 2, SUB, PHASE), BF16),
        pltpu.VMEM((2, NX - 1, 2, SUB, PHASE), BF16),
        pltpu.VMEM((2, NX - 1, 2, SUB, PHASE), BF16),
        pltpu.VMEM((2, 2, SUB, PHASE), F32),
        pltpu.VMEM((2, 2, SUB, PHASE), BF16),
        pltpu.VMEM((2, 2, 2, NZH, SUB, PHASE), BF16),
        pltpu.VMEM((2, 2, NX, SUB, PHASE), BF16),
        pltpu.VMEM((NZH, 2, NX, SUB, 128), BF16),
        pltpu.VMEM((NZH, 2, NX, SUB, 128), BF16),
        pltpu.VMEM((2, 2, 2, NY, 32, HALF), F32),
        pltpu.VMEM((2, 2, NY, 32, HALF), BF16),
        pltpu.VMEM((2, 2, NY, 32, HALF), BF16),
        pltpu.VMEM((2, NX, 2, NY, 32, 128), BF16),
        pltpu.VMEM((2, NX - 1, 2, NY, 32, 128), BF16),
        pltpu.VMEM((2, 2, NY, 32, 128), BF16),
        pltpu.VMEM((NZH, NY, 32, 128), BF16),
        pltpu.SemaphoreType.DMA((5,)),
        pltpu.SemaphoreType.DMA((COPIES,)),
        pltpu.SemaphoreType.DMA((COPIES,)),
    ]
    token_grad, weight_grad, down_grad = pl.pallas_call(
        kernel,
        out_shape=between,
        in_specs=[hbm] * 5,
        out_specs=[vmem] * 3,
        scratch_shapes=scratch,
        compiler_params=pltpu.CompilerParams(
            collective_id=0, has_side_effects=True, vmem_limit_bytes=60 * 2**20
        ),
        name="layer",
    )(tokens, cotangent, gate_weight, up_weight, down_weight)
    return pl.pallas_call(
        finish,
        out_shape=outs,
        in_specs=[hbm] * 3,
        out_specs=[hbm] * 4,
        scratch_shapes=[
            pltpu.VMEM(tokens.shape, F32),
            pltpu.VMEM((NZH, 896, 128), BF16),
            pltpu.VMEM(down_weight.shape, F32),
            pltpu.VMEM(gate_weight.shape, F32),
            pltpu.VMEM(up_weight.shape, F32),
            pltpu.SemaphoreType.DMA((NZH + 2 + 2 * NZH + 2,)),
        ],
        compiler_params=pltpu.CompilerParams(vmem_limit_bytes=60 * 2**20),
        name="finish",
    )(token_grad, weight_grad, down_grad)


def solution(mesh):
    return jax.shard_map(
        shards,
        mesh=mesh,
        in_specs=(
            P(("dep", "out"), "inp"),
            P(("dep", "out"), "inp"),
            P(("inp", "dep"), "out"),
            P(("inp", "dep"), "out"),
            P(("out", "dep"), "inp"),
        ),
        out_specs=(
            P(("dep", "out"), "inp"),
            P(("inp", "dep"), "out"),
            P(("inp", "dep"), "out"),
            P(("out", "dep"), "inp"),
        ),
        check_vma=False,
    )
```

time: 102 us -> 93.3 us (0.915)
  Pallas kernels: 101 us -> 92.5 us
    pallas_call x1, Pallas kernels: 97.6 us -> 89.5 us  [shards(): pl.pallas_call(kernel, out_shape=between, in_specs=[hbm] * 5, out_specs=[...]
where the time goes in v4:
time: 93.3 us; the launch traced here: 93.1 us
  Pallas kernels  92.5 us (99%)
    pallas_call x1, Pallas kernels, shards(): pl.pallas_call(kernel, out_shape=between, in_specs=[hbm] * 5, out_specs=[...  89.5 us
    pallas_call x1, Pallas kernels, shards(): pl.pallas_call(finish, out_shape=outs, in_specs=[hbm] * 3, out_specs=[hbm...  2.98 us

profile of v4, /device:TPU:1, one launch (start us, length us, event | category | flops | bytes accessed | tf_op | source)
XLA Modules:
  0.0 93.1 jit_solution(14140080179227492529)
XLA Ops:
  0.6 89.5 %layer.1 = (f32[32,512]{1,0:T(8,128)}, bf16[4,896,128]{2,1,0:T(8,128)(2,1)}, f32[448,512]{1,0:T(8,128)}) custom-call(bf16[32,512]{1,0:T(8,128)(2,1)} %tok_hbm.1, bf16[32,512]{1,0:T(8,128)(2,1)} %cot_hbm.1, bf16[64,3584]{1,0:T(8,128)(2,1)} %gate_hbm.1, bf16[64,3584]{1,0:T(8,128)(2,1)} %up_hbm.1, bf16[448,512]{1,0:T(8,128)(2,1)} %down_hbm.1), custom_call_target="tpu_custom_call" | custom-call | tf_op jit(solution)/shard_map/layer/pallas_call | solution.py:428
  90.2 3.0 %finish.1 = (f32[32,512]{1,0:T(8,128)}, f32[64,3584]{1,0:T(8,128)}, f32[64,3584]{1,0:T(8,128)}, f32[448,512]{1,0:T(8,128)}) custom-call(f32[32,512]{1,0:T(8,128)} %get-tuple-element.7.tg_in, bf16[4,896,128]{2,1,0:T(8,128)(2,1)} %get-tuple-element.8.wg_in, f32[448,512]{1,0:T(8,128)} %get-tuple-element.9.down_in), custom_call_target="tpu_custom_call" | custom-call | tf_op jit(solution)/shard_map/finish/pallas_call | solution.py:439

commit v5 on v4

--- a/solution.py
+++ b/solution.py
@@ -45,6 +45,7 @@
     tok_in, cot_in, gate_in, up_in, down_in,
     wt, wblk, gu, tok, cot, rs_send, rs_recv, hg_send, hg_recv, hg_own, pair,
     grads, hid, wg_send, wg_recv, part, ta_send, ta_recv, tb_send, tb_recv, tc_send, tc_recv,
+    down_grad, token_grad,
     load_sems, send_sems, recv_sems,
 ):
     inp, y, dep = lax.axis_index("inp"), lax.axis_index("out"), lax.axis_index("dep")
@@ -74,8 +75,7 @@
         loads.append(pltpu.make_async_copy(src, dst, load_sems.at[len(loads)]))
         loads[-1].start()
 
-    peers = [at(zh_=zhs[m], y_=ys[k]) for m in range(1, NZH) for k in range(NY)]
-    peers += [at(x_=xs[k], zh_=zhs[m]) for m in range(1, NZH) for k in range(1, NX)]
+    peers = [at(x_=xs[k], zh_=zhs[m]) for m in range(1, NZH) for k in range(NX)]
     peers += around
     peers += [at(y_=ys[k]) for k in range(1, NY)]
     peers += [at(x_=xs[k], c_=cs[e]) for k in range(1, NX) for e in range(2)]
@@ -121,7 +121,7 @@
         )
         for m in (2, 1, 3, 0) for k in (2, 1, 3, 0) if (m, k) != (0, 0)
     ]
-    cot_first = [send(cot_in, cot.at[zh // 2, zh % 2, c, y], at(zh_=zhs[m])) for m in (2, 1, 3)]
+    cot_first = [send(cot_in, cot.at[zh // 2, zh % 2, c, y], at(y_=ys[k])) for k in (2, 1, 3)]
 
     def send_weights(q):
         return [
@@ -129,23 +129,25 @@
             for k in (2, 1, 3, 0) for e in range(2) if (k, e) != (0, 0)
         ]
 
-    def spread(buffer, p):
-        own = buffer.at[:, p, c, y]
+    def spread(p):
+        own = tok.at[:, p, c, y]
         return {k: send(own, own, at(y_=ys[k])) for k in (2, 1, 3)}, [send(own, own, at(c_=cs[1]))]
 
-    def share(buffer, p, by_y, by_core):
+    def share(p, by_y, by_core):
         for k in (1, 3, 2):
             by_y[k].wait_recv()
-            rows = buffer.at[:, p, c, ys[NY - k]]
+            rows = tok.at[:, p, c, ys[NY - k]]
             by_core.append(send(rows, rows, at(c_=cs[1])))
         arrive(by_core)
 
     order = [zhs[2], zhs[1], zhs[3], zhs[0]]
     weights = [send_weights(order[0])]
+    arrive(cot_first)
+    own = cot.at[zh // 2, zh % 2, c]
+    cot_z = {m: send(own, own, at(zh_=zhs[m])) for m in (2, 1, 3)}
+    cot_core = [send(own, own, at(c_=cs[1]))]
     arrive(tok_first)
-    tok_later = [spread(tok, p) for p in range(2)]
-    arrive(cot_first)
-    cot_later = [spread(cot, p) for p in range(2)]
+    tok_later = [spread(p) for p in range(2)]
     for q in range(1, NZH):
         weights.append(send_weights(order[q]))
 
@@ -194,7 +196,6 @@
         return nt(rows, cot[:, p].reshape(2 * PHASE, HALF))
 
     def hidden_over_x(p):
-        share(cot, p, *cot_later[p])
         copies = []
         for k in (2, 1, 3):
             some = hidden_part(xs[k], p).astype(BF16)
@@ -220,13 +221,20 @@
     assemble(0)
     moving, by_x, by_pair = [None, None], [None, None], [None, None]
     for p in range(2):
-        share(tok, p, *tok_later[p])
+        share(p, *tok_later[p])
         moving[p] = outset(p)
     assemble(1)
     assemble(2)
-    for p in range(2):
-        moving[p] = onward(1, p, moving[p])
-        by_x[p] = hidden_over_x(p)
+    moving[0] = onward(1, 0, moving[0])
+    for m in (1, 3, 2):
+        cot_z[m].wait_recv()
+        there = zhs[NZH - m]
+        rows = cot.at[there // 2, there % 2, c]
+        cot_core.append(send(rows, rows, at(c_=cs[1])))
+    arrive(cot_core)
+    by_x[0] = hidden_over_x(0)
+    moving[1] = onward(1, 1, moving[1])
+    by_x[1] = hidden_over_x(1)
     assemble(3)
     for p in range(2):
         moving[p] = onward(2, p, moving[p])
@@ -262,7 +270,7 @@
         hid[zl, p, x] = hidden
         by_pair[p] = send(hid.at[zl, p, x], hid.at[zl, p, x], partner)
 
-    returned = []
+    returned = {}
 
     def weight_grads(q):
         both = jnp.zeros((2 * SUB, HALF), F32)
@@ -276,12 +284,10 @@
             wg_send[q, 0, k] = jnp.concatenate((here[:SUB, :64], here[SUB:, :64]), axis=1)
             wg_send[q, 1, k] = jnp.concatenate((here[:SUB, 64:], here[SUB:, 64:]), axis=1)
         wg_recv[q, c, x] = wg_send[q, c, x]
-        for k in (2, 1, 3, 0):
-            for e in range(2):
-                if (k, e) != (0, 0):
-                    returned.append(
-                        send(wg_send.at[q, cs[e], xs[k]], wg_recv.at[q, c, x], at(x_=xs[k], c_=cs[e]))
-                    )
+        return [
+            send(wg_send.at[q, cs[e], xs[k]], wg_recv.at[q, c, x], at(x_=xs[k], c_=cs[e]))
+            for k in (2, 1, 3, 0) for e in range(2) if (k, e) != (0, 0)
+        ]
 
     def over_core(p):
         for half in range(2):
@@ -290,20 +296,21 @@
         ta_send[p] = part[p, :, cs[1]].astype(BF16)
         return send(ta_send.at[p], ta_recv.at[p], at(c_=cs[1]))
 
-    def over_x(p, by_core):
+    def over_y(p, by_core):
         by_core.wait_recv()
         total = part[p, :, c] + ta_recv[p].astype(F32)
         part[p, :, c] = total
+        for k in range(NY):
+            tb_send[p, k] = total[:, k].astype(BF16)
+        return [send(tb_send.at[p, ys[k]], tb_recv.at[p, k - 1], at(y_=ys[k])) for k in (2, 1, 3)]
+
+    def sum_y(p, by_y):
+        arrive(by_y)
+        total = part[p, :, c, y]
+        for k in range(NY - 1):
+            total = total + tb_recv[p, k].astype(F32)
         for k in range(NX):
-            tb_send[p, k] = total[:, :, :, k * 128 : (k + 1) * 128].astype(BF16)
-        return [send(tb_send.at[p, xs[k]], tb_recv.at[p, k - 1], at(x_=xs[k])) for k in (2, 1, 3)]
-
-    def sum_x(p, by_x):
-        arrive(by_x)
-        total = part[p, :, c, :, :, lanes(x)]
-        for k in range(NX - 1):
-            total = total + tb_recv[p, k].astype(F32)
-        tc_send[:, p] = total.astype(BF16)
+            tc_send[:, p, k] = total[:, :, k * 128 : (k + 1) * 128].astype(BF16)
 
     turn = 2 * zl - 1
     finished = [zh, (zh + turn + NZH) % NZH, (zh - turn + NZH) % NZH, zhs[2]]
@@ -313,24 +320,29 @@
             moving[p] = forward(step + 1, p)
             if step == 0:
                 by_pair[p].wait_recv()
-                by_x[p] = [send(hid.at[:, p, x], hid.at[:, p, x], at(x_=xs[k])) for k in (2, 1, 3)]
-        if step < 2:
-            weight_grads(finished[step])
+                own = hid.at[:, p, x]
+                by_x[p] = {k: send(own, own, at(x_=xs[k])) for k in (1, 3)}
+            if step == 1:
+                arrive(by_x[p].values())
+                by_x[p] = []
+                for half, k in ((0, 1), (1, 3)):
+                    passed = hid.at[half, p, xs[NX - k]]
+                    by_x[p].append(send(passed, passed, at(x_=xs[k])))
+        returned[step] = weight_grads(finished[step])
     arrive(moving[0])
-    early = over_x(0, over_core(0))
+    early = over_y(0, over_core(0))
     arrive(moving[1])
-    late = over_x(1, over_core(1))
-    weight_grads(finished[2])
-    weight_grads(finished[3])
-    sum_x(0, early)
-    sum_x(1, late)
+    late = over_y(1, over_core(1))
+    returned[3] = weight_grads(finished[3])
+    sum_y(0, early)
+    sum_y(1, late)
     by_place = [
         send(
-            tc_send.at[zhs[m] // 2, zhs[m] % 2, ys[k]], tc_recv.at[zh, k], at(zh_=zhs[m], y_=ys[k])
+            tc_send.at[zhs[m] // 2, zhs[m] % 2, xs[k]], tc_recv.at[zh, k], at(zh_=zhs[m], x_=xs[k])
         )
         for m in (2, 1, 3, 0) for k in (2, 1, 3, 0) if (m, k) != (0, 0)
     ]
-    tc_recv[zh, 0] = tc_send[zh // 2, zh % 2, y]
+    tc_recv[zh, 0] = tc_send[zh // 2, zh % 2, x]
     arrive(by_x[0])
     arrive(by_x[1])
     down = jnp.zeros((4 * SUB, HALF), F32)
@@ -338,17 +350,28 @@
         for p in range(2):
             rows = hid[half, p].reshape(4 * SUB, PHASE)
             down = down + nn(rows, cot[half, p].reshape(PHASE, HALF))
-    down_out[...] = down
-    arrive(returned)
-    wg_out[...] = wg_recv[...].reshape(NZH, 896, 128)
+    down_grad[...] = down
+    stores = []
+
+    def store(src, dst):
+        stores.append(pltpu.make_async_copy(src, dst, load_sems.at[len(loads) + len(stores)]))
+        stores[-1].start()
+
+    store(down_grad, down_out)
+    for step in range(4):
+        arrive(returned[step])
+        store(wg_recv.at[finished[step]], wg_out.at[finished[step]])
     arrive(by_place)
     for q in range(NZH):
         total = tc_recv[q, 0].astype(F32)
-        for k in range(1, NY):
+        for k in range(1, NX):
             total = total + tc_recv[q, k].astype(F32)
-        tg_out[:, pl.ds(q * 128, 128)] = total
+        token_grad[:, pl.ds(q * 128, 128)] = total
+    store(token_grad, tg_out)
     for copy in started:
         copy.wait_send()
+    for copy in stores:
+        copy.wait()
 
 
 def finish(tg_in, wg_in, down_in, tg_out, gate_out, up_out, down_out, tg, wg, down, gate, up, sems):
@@ -366,7 +389,7 @@
     for q in range(NZH):
         loads[q].wait()
         here = pl.ds(q * 896, 896)
-        block = wg[q].T.astype(F32)
+        block = wg[q].reshape(896, 128).T.astype(F32)
         for rows, buffer, out in ((block[:64], gate, gate_out), (block[64:], up, up_out)):
             buffer[:, here] = rows
             store(buffer.at[:, here], out.at[:, here])
@@ -380,7 +403,6 @@
 
 
 def shards(tokens, cotangent, gate_weight, up_weight, down_weight):
-    vmem = pl.BlockSpec(memory_space=pltpu.VMEM)
     hbm = pl.BlockSpec(memory_space=pltpu.HBM)
     outs = [
         jax.ShapeDtypeStruct(tokens.shape, F32),
@@ -390,7 +412,7 @@
     ]
     between = [
         outs[0],
-        jax.ShapeDtypeStruct((NZH, 896, 128), BF16),
+        jax.ShapeDtypeStruct((NZH, 2, NX, SUB, 128), BF16),
         outs[3],
     ]
     scratch = [
@@ -417,11 +439,13 @@
         pltpu.VMEM((2, 2, 2, NY, 32, HALF), F32),
         pltpu.VMEM((2, 2, NY, 32, HALF), BF16),
         pltpu.VMEM((2, 2, NY, 32, HALF), BF16),
-        pltpu.VMEM((2, NX, 2, NY, 32, 128), BF16),
-        pltpu.VMEM((2, NX - 1, 2, NY, 32, 128), BF16),
-        pltpu.VMEM((2, 2, NY, 32, 128), BF16),
-        pltpu.VMEM((NZH, NY, 32, 128), BF16),
-        pltpu.SemaphoreType.DMA((5,)),
+        pltpu.VMEM((2, NY, 2, 32, HALF), BF16),
+        pltpu.VMEM((2, NY - 1, 2, 32, HALF), BF16),
+        pltpu.VMEM((2, 2, NX, 32, 128), BF16),
+        pltpu.VMEM((NZH, NX, 32, 128), BF16),
+        pltpu.VMEM(down_weight.shape, F32),
+        pltpu.VMEM(tokens.shape, F32),
+        pltpu.SemaphoreType.DMA((11,)),
         pltpu.SemaphoreType.DMA((COPIES,)),
         pltpu.SemaphoreType.DMA((COPIES,)),
     ]
@@ -429,7 +453,7 @@
         kernel,
         out_shape=between,
         in_specs=[hbm] * 5,
-        out_specs=[vmem] * 3,
+        out_specs=[hbm] * 3,
         scratch_shapes=scratch,
         compiler_params=pltpu.CompilerParams(
             collective_id=0, has_side_effects=True, vmem_limit_bytes=60 * 2**20
@@ -443,7 +467,7 @@
         out_specs=[hbm] * 4,
         scratch_shapes=[
             pltpu.VMEM(tokens.shape, F32),
-            pltpu.VMEM((NZH, 896, 128), BF16),
+            pltpu.VMEM((NZH, 2, NX, SUB, 128), BF16),
             pltpu.VMEM(down_weight.shape, F32),
             pltpu.VMEM(gate_weight.shape, F32),
             pltpu.VMEM(up_weight.shape, F32),

time: 93.3 us -> 91.3 us (0.979)
  Pallas kernels: 92.5 us -> 90.6 us
    pallas_call x1, Pallas kernels: 89.5 us -> 87.6 us  [shards(): pl.pallas_call(kernel, out_shape=between, in_specs=[hbm] * 5, out_specs=[...]
where the time goes in v5:
time: 91.3 us; the launch traced here: 91.2 us
  Pallas kernels  90.6 us (99%)
    pallas_call x1, Pallas kernels, shards(): pl.pallas_call(kernel, out_shape=between, in_specs=[hbm] * 5, out_specs=[...  87.6 us
    pallas_call x1, Pallas kernels, shards(): pl.pallas_call(finish, out_shape=outs, in_specs=[hbm] * 3, out_specs=[hbm...  2.98 us

profile of v5, /device:TPU:1, one launch (start us, length us, event | category | flops | bytes accessed | tf_op | source)
XLA Modules:
  0.0 91.2 jit_solution(11234025321807357548)
XLA Ops:
  0.6 87.6 %layer.1 = (f32[32,512]{1,0:T(8,128)}, bf16[4,2,4,112,128]{4,3,2,1,0:T(8,128)(2,1)}, f32[448,512]{1,0:T(8,128)}) custom-call(bf16[32,512]{1,0:T(8,128)(2,1)} %tok_hbm.1, bf16[32,512]{1,0:T(8,128)(2,1)} %cot_hbm.1, bf16[64,3584]{1,0:T(8,128)(2,1)} %gate_hbm.1, bf16[64,3584]{1,0:T(8,128)(2,1)} %up_hbm.1, bf16[448,512]{1,0:T(8,128)(2,1)} %down_hbm.1), custom_call_target="tpu_custom_call" | custom-call | tf_op jit(solution)/shard_map/layer/pallas_call | solution.py:452
  88.2 3.0 %finish.1 = (f32[32,512]{1,0:T(8,128)}, f32[64,3584]{1,0:T(8,128)}, f32[64,3584]{1,0:T(8,128)}, f32[448,512]{1,0:T(8,128)}) custom-call(f32[32,512]{1,0:T(8,128)} %get-tuple-element.7.tg_in, bf16[4,2,4,112,128]{4,3,2,1,0:T(8,128)(2,1)} %get-tuple-element.8.wg_in, f32[448,512]{1,0:T(8,128)} %get-tuple-element.9.down_in), custom_call_target="tpu_custom_call" | custom-call | tf_op jit(solution)/shard_map/finish/pallas_call | solution.py:463

commit v6 on v5

--- a/solution.py
+++ b/solution.py
@@ -11,7 +11,7 @@
 SUB = 112
 HALF = 512
 PHASE = 256
-COPIES = 180
+COPIES = 190
 
 
 def nt(left_side, right_side):
@@ -122,6 +122,8 @@
         for m in (2, 1, 3, 0) for k in (2, 1, 3, 0) if (m, k) != (0, 0)
     ]
     cot_first = [send(cot_in, cot.at[zh // 2, zh % 2, c, y], at(y_=ys[k])) for k in (2, 1, 3)]
+    far = zhs[2]
+    cot_far = send(cot_in, cot.at[zh // 2, zh % 2, c, y], at(zh_=far))
 
     def send_weights(q):
         return [
@@ -144,10 +146,14 @@
     weights = [send_weights(order[0])]
     arrive(cot_first)
     own = cot.at[zh // 2, zh % 2, c]
-    cot_z = {m: send(own, own, at(zh_=zhs[m])) for m in (2, 1, 3)}
+    cot_z = {m: send(own, own, at(zh_=zhs[m])) for m in (1, 3)}
     cot_core = [send(own, own, at(c_=cs[1]))]
     arrive(tok_first)
     tok_later = [spread(p) for p in range(2)]
+    cot_far.wait_recv()
+    own = cot.at[far // 2, far % 2, c, y]
+    cot_y = {k: send(own, own, at(y_=ys[k])) for k in (2, 1, 3)}
+    cot_core.append(send(own, own, at(c_=cs[1])))
     for q in range(1, NZH):
         weights.append(send_weights(order[q]))
 
@@ -226,10 +232,14 @@
     assemble(1)
     assemble(2)
     moving[0] = onward(1, 0, moving[0])
-    for m in (1, 3, 2):
+    for m in (1, 3):
         cot_z[m].wait_recv()
         there = zhs[NZH - m]
         rows = cot.at[there // 2, there % 2, c]
+        cot_core.append(send(rows, rows, at(c_=cs[1])))
+    for k in (1, 3, 2):
+        cot_y[k].wait_recv()
+        rows = cot.at[far // 2, far % 2, c, ys[NY - k]]
         cot_core.append(send(rows, rows, at(c_=cs[1])))
     arrive(cot_core)
     by_x[0] = hidden_over_x(0)
@@ -268,7 +278,6 @@
         grads[zl, p, 1, zh] = up_grad
         moving[p] = forward(0, p)
         hid[zl, p, x] = hidden
-        by_pair[p] = send(hid.at[zl, p, x], hid.at[zl, p, x], partner)
 
     returned = {}
 
@@ -318,22 +327,25 @@
         for p in range(2):
             arrive(moving[p])
             moving[p] = forward(step + 1, p)
-            if step == 0:
-                by_pair[p].wait_recv()
-                own = hid.at[:, p, x]
-                by_x[p] = {k: send(own, own, at(x_=xs[k])) for k in (1, 3)}
-            if step == 1:
-                arrive(by_x[p].values())
-                by_x[p] = []
-                for half, k in ((0, 1), (1, 3)):
-                    passed = hid.at[half, p, xs[NX - k]]
-                    by_x[p].append(send(passed, passed, at(x_=xs[k])))
         returned[step] = weight_grads(finished[step])
+    by_pair = [send(hid.at[zl, p, x], hid.at[zl, p, x], partner) for p in range(2)]
     arrive(moving[0])
-    early = over_y(0, over_core(0))
+    by_core = over_core(0)
+    for p in range(2):
+        by_pair[p].wait_recv()
+        own = hid.at[:, p, x]
+        by_x[p] = {k: send(own, own, at(x_=xs[k])) for k in (1, 3)}
+    early = over_y(0, by_core)
     arrive(moving[1])
-    late = over_y(1, over_core(1))
+    by_core = over_core(1)
     returned[3] = weight_grads(finished[3])
+    late = over_y(1, by_core)
+    for p in range(2):
+        arrive(by_x[p].values())
+        by_x[p] = []
+        for half, k in ((0, 1), (1, 3)):
+            passed = hid.at[half, p, xs[NX - k]]
+            by_x[p].append(send(passed, passed, at(x_=xs[k])))
     sum_y(0, early)
     sum_y(1, late)
     by_place = [

time: 91.3 us -> 89 us (0.975)
  Pallas kernels: 90.6 us -> 88.3 us
    pallas_call x1, Pallas kernels: 87.6 us -> 85.3 us  [shards(): pl.pallas_call(kernel, out_shape=between, in_specs=[hbm] * 5, out_specs=[...]
where the time goes in v6:
time: 89 us; the launch traced here: 88.9 us
  Pallas kernels  88.3 us (99%)
    pallas_call x1, Pallas kernels, shards(): pl.pallas_call(kernel, out_shape=between, in_specs=[hbm] * 5, out_specs=[...  85.3 us
    pallas_call x1, Pallas kernels, shards(): pl.pallas_call(finish, out_shape=outs, in_specs=[hbm] * 3, out_specs=[hbm...  2.98 us

profile of v6, /device:TPU:1, one launch (start us, length us, event | category | flops | bytes accessed | tf_op | source)
XLA Modules:
  0.0 88.9 jit_solution(18253801636181319695)
XLA Ops:
  0.6 85.3 %layer.1 = (f32[32,512]{1,0:T(8,128)}, bf16[4,2,4,112,128]{4,3,2,1,0:T(8,128)(2,1)}, f32[448,512]{1,0:T(8,128)}) custom-call(bf16[32,512]{1,0:T(8,128)(2,1)} %tok_hbm.1, bf16[32,512]{1,0:T(8,128)(2,1)} %cot_hbm.1, bf16[64,3584]{1,0:T(8,128)(2,1)} %gate_hbm.1, bf16[64,3584]{1,0:T(8,128)(2,1)} %up_hbm.1, bf16[448,512]{1,0:T(8,128)(2,1)} %down_hbm.1), custom_call_target="tpu_custom_call" | custom-call | tf_op jit(solution)/shard_map/layer/pallas_call | solution.py:464
  85.9 3.0 %finish.1 = (f32[32,512]{1,0:T(8,128)}, f32[64,3584]{1,0:T(8,128)}, f32[64,3584]{1,0:T(8,128)}, f32[448,512]{1,0:T(8,128)}) custom-call(f32[32,512]{1,0:T(8,128)} %get-tuple-element.7.tg_in, bf16[4,2,4,112,128]{4,3,2,1,0:T(8,128)(2,1)} %get-tuple-element.8.wg_in, f32[448,512]{1,0:T(8,128)} %get-tuple-element.9.down_in), custom_call_target="tpu_custom_call" | custom-call | tf_op jit(solution)/shard_map/finish/pallas_call | solution.py:475

commit v7 on v6

--- a/solution.py
+++ b/solution.py
@@ -11,7 +11,7 @@
 SUB = 112
 HALF = 512
 PHASE = 256
-COPIES = 190
+COPIES = 200
 
 
 def nt(left_side, right_side):
@@ -43,7 +43,7 @@
     tok_hbm, cot_hbm, gate_hbm, up_hbm, down_hbm,
     tg_out, wg_out, down_out,
     tok_in, cot_in, gate_in, up_in, down_in,
-    wt, wblk, gu, tok, cot, rs_send, rs_recv, hg_send, hg_recv, hg_own, pair,
+    wt, wblk, gu, tok, cot, rs_send, rs_recv, hg_send, hg_recv, pair,
     grads, hid, wg_send, wg_recv, part, ta_send, ta_recv, tb_send, tb_recv, tc_send, tc_recv,
     down_grad, token_grad,
     load_sems, send_sems, recv_sems,
@@ -182,7 +182,10 @@
         return row
 
     def onward(step, p, row):
-        terms = [partial(ring(4 - step), p), partial(ring(step - 4), p)]
+        there = [ring(4 - step), ring(step - 4)]
+        rows = [gu[:, one[0]].reshape(2 * SUB, HALF) for one in there]
+        both = nt(jnp.concatenate(rows, axis=0), tok[there[0][1], p].reshape(PHASE, HALF))
+        terms = both.reshape(2, 2, SUB, PHASE)
         later = []
         for d in range(2):
             row[d].wait_recv()
@@ -197,24 +200,15 @@
             later.append(send(rs_send.at[p, d, step], rs_recv.at[p, d, step], around[d]))
         return later
 
-    def hidden_part(q, p):
-        rows = down_in[pl.ds(pl.multiple_of(q * SUB, 16), SUB), :]
-        return nt(rows, cot[:, p].reshape(2 * PHASE, HALF))
-
     def hidden_over_x(p):
-        copies = []
-        for k in (2, 1, 3):
-            some = hidden_part(xs[k], p).astype(BF16)
-            for half in range(2):
-                hg_send[p, k - 1, half] = some[:, half * PHASE : (half + 1) * PHASE]
-            copies.append(send(hg_send.at[p, k - 1], hg_recv.at[p, k - 1], at(x_=xs[k])))
-        some = hidden_part(x, p)
+        full = nt(down_in[...], cot[:, p].reshape(2 * PHASE, HALF)).astype(BF16)
         for half in range(2):
-            hg_own[p, half] = some[:, half * PHASE : (half + 1) * PHASE]
-        return copies
+            some = full[:, half * PHASE : (half + 1) * PHASE]
+            hg_send[p, :, half] = some.reshape(NX, SUB, PHASE)
+        return [send(hg_send.at[p, xs[k]], hg_recv.at[p, k - 1], at(x_=xs[k])) for k in (2, 1, 3)]
 
     def hidden_sum(p, half):
-        total = hg_own[p, half]
+        total = hg_send[p, x, half].astype(F32)
         for k in range(NX - 1):
             total = total + hg_recv[p, k, half].astype(F32)
         return total
@@ -298,28 +292,28 @@
             for k in (2, 1, 3, 0) for e in range(2) if (k, e) != (0, 0)
         ]
 
-    def over_core(p):
-        for half in range(2):
-            term = tn(grads[half, p].reshape(8 * SUB, PHASE), gu[...].reshape(8 * SUB, HALF))
-            part[p, half] = term.reshape(2, NY, 32, HALF)
-        ta_send[p] = part[p, :, cs[1]].astype(BF16)
-        return send(ta_send.at[p], ta_recv.at[p], at(c_=cs[1]))
-
-    def over_y(p, by_core):
+    def over_core(half, p):
+        term = tn(grads[half, p].reshape(8 * SUB, PHASE), gu[...].reshape(8 * SUB, HALF))
+        part[half, p] = term.reshape(2, NY, 32, HALF)
+        ta_send[half, p] = part[half, p, cs[1]].astype(BF16)
+        return send(ta_send.at[half, p], ta_recv.at[half, p], at(c_=cs[1]))
+
+    def over_y(half, p, by_core):
         by_core.wait_recv()
-        total = part[p, :, c] + ta_recv[p].astype(F32)
-        part[p, :, c] = total
-        for k in range(NY):
-            tb_send[p, k] = total[:, k].astype(BF16)
-        return [send(tb_send.at[p, ys[k]], tb_recv.at[p, k - 1], at(y_=ys[k])) for k in (2, 1, 3)]
-
-    def sum_y(p, by_y):
+        total = part[half, p, c] + ta_recv[half, p].astype(F32)
+        part[half, p, c] = total
+        tb_send[half, p] = total.astype(BF16)
+        return [
+            send(tb_send.at[half, p, ys[k]], tb_recv.at[half, p, k - 1], at(y_=ys[k])) for k in (2, 1, 3)
+        ]
+
+    def sum_y(half, p, by_y):
         arrive(by_y)
-        total = part[p, :, c, y]
+        total = part[half, p, c, y]
         for k in range(NY - 1):
-            total = total + tb_recv[p, k].astype(F32)
+            total = total + tb_recv[half, p, k].astype(F32)
         for k in range(NX):
-            tc_send[:, p, k] = total[:, :, k * 128 : (k + 1) * 128].astype(BF16)
+            tc_send[half, p, k] = total[:, k * 128 : (k + 1) * 128].astype(BF16)
 
     turn = 2 * zl - 1
     finished = [zh, (zh + turn + NZH) % NZH, (zh - turn + NZH) % NZH, zhs[2]]
@@ -329,25 +323,29 @@
             moving[p] = forward(step + 1, p)
         returned[step] = weight_grads(finished[step])
     by_pair = [send(hid.at[zl, p, x], hid.at[zl, p, x], partner) for p in range(2)]
+    early = [over_core(1 - zl, p) for p in range(2)]
+    early = [over_y(1 - zl, p, early[p]) for p in range(2)]
     arrive(moving[0])
-    by_core = over_core(0)
+    by_core = over_core(zl, 0)
     for p in range(2):
         by_pair[p].wait_recv()
         own = hid.at[:, p, x]
         by_x[p] = {k: send(own, own, at(x_=xs[k])) for k in (1, 3)}
-    early = over_y(0, by_core)
+    late = [over_y(zl, 0, by_core)]
     arrive(moving[1])
-    by_core = over_core(1)
+    by_core = over_core(zl, 1)
     returned[3] = weight_grads(finished[3])
-    late = over_y(1, by_core)
+    late.append(over_y(zl, 1, by_core))
     for p in range(2):
         arrive(by_x[p].values())
         by_x[p] = []
         for half, k in ((0, 1), (1, 3)):
             passed = hid.at[half, p, xs[NX - k]]
             by_x[p].append(send(passed, passed, at(x_=xs[k])))
-    sum_y(0, early)
-    sum_y(1, late)
+    for p in range(2):
+        sum_y(1 - zl, p, early[p])
+    for p in range(2):
+        sum_y(zl, p, late[p])
     by_place = [
         send(
             tc_send.at[zhs[m] // 2, zhs[m] % 2, xs[k]], tc_recv.at[zh, k], at(zh_=zhs[m], x_=xs[k])
@@ -440,9 +438,8 @@
         pltpu.VMEM((2, 2, 2, NY, 32, HALF), BF16),
         pltpu.VMEM((2, 2, 4, 2, SUB, PHASE), BF16),
         pltpu.VMEM((2, 2, 4, 2, SUB, PHASE), BF16),
+        pltpu.VMEM((2, NX, 2, SUB, PHASE), BF16),
         pltpu.VMEM((2, NX - 1, 2, SUB, PHASE), BF16),
-        pltpu.VMEM((2, NX - 1, 2, SUB, PHASE), BF16),
-        pltpu.VMEM((2, 2, SUB, PHASE), F32),
         pltpu.VMEM((2, 2, SUB, PHASE), BF16),
         pltpu.VMEM((2, 2, 2, NZH, SUB, PHASE), BF16),
         pltpu.VMEM((2, 2, NX, SUB, PHASE), BF16),
@@ -451,8 +448,8 @@
         pltpu.VMEM((2, 2, 2, NY, 32, HALF), F32),
         pltpu.VMEM((2, 2, NY, 32, HALF), BF16),
         pltpu.VMEM((2, 2, NY, 32, HALF), BF16),
-        pltpu.VMEM((2, NY, 2, 32, HALF), BF16),
-        pltpu.VMEM((2, NY - 1, 2, 32, HALF), BF16),
+        pltpu.VMEM((2, 2, NY, 32, HALF), BF16),
+        pltpu.VMEM((2, 2, NY - 1, 32, HALF), BF16),
         pltpu.VMEM((2, 2, NX, 32, 128), BF16),
         pltpu.VMEM((NZH, NX, 32, 128), BF16),
         pltpu.VMEM(down_weight.shape, F32),

time: 89 us -> 88.9 us (level); the launches traced: 88.9 us -> 87.7 us
  Pallas kernels: 88.3 us -> 87 us
    pallas_call x1, Pallas kernels: 85.3 us -> 84 us  [shards(): pl.pallas_call(kernel, out_shape=between, in_specs=[hbm] * 5, out_specs=[...]
where the time goes in v7:
time: 88.9 us; the launch traced here: 87.7 us
  Pallas kernels  87 us (98%)
    pallas_call x1, Pallas kernels, shards(): pl.pallas_call(kernel, out_shape=between, in_specs=[hbm] * 5, out_specs=[...  84 us
    pallas_call x1, Pallas kernels, shards(): pl.pallas_call(finish, out_shape=outs, in_specs=[hbm] * 3, out_specs=[hbm...  2.98 us

profile of v7, /device:TPU:1, one launch (start us, length us, event | category | flops | bytes accessed | tf_op | source)
XLA Modules:
  0.0 87.7 jit_solution(16340614166722553011)
XLA Ops:
  0.6 84.0 %layer.1 = (f32[32,512]{1,0:T(8,128)}, bf16[4,2,4,112,128]{4,3,2,1,0:T(8,128)(2,1)}, f32[448,512]{1,0:T(8,128)}) custom-call(bf16[32,512]{1,0:T(8,128)(2,1)} %tok_hbm.1, bf16[32,512]{1,0:T(8,128)(2,1)} %cot_hbm.1, bf16[64,3584]{1,0:T(8,128)(2,1)} %gate_hbm.1, bf16[64,3584]{1,0:T(8,128)(2,1)} %up_hbm.1, bf16[448,512]{1,0:T(8,128)(2,1)} %down_hbm.1), custom_call_target="tpu_custom_call" | custom-call | tf_op jit(solution)/shard_map/layer/pallas_call | solution.py:461
  84.7 3.0 %finish.1 = (f32[32,512]{1,0:T(8,128)}, f32[64,3584]{1,0:T(8,128)}, f32[64,3584]{1,0:T(8,128)}, f32[448,512]{1,0:T(8,128)}) custom-call(f32[32,512]{1,0:T(8,128)} %get-tuple-element.7.tg_in, bf16[4,2,4,112,128]{4,3,2,1,0:T(8,128)(2,1)} %get-tuple-element.8.wg_in, f32[448,512]{1,0:T(8,128)} %get-tuple-element.9.down_in), custom_call_target="tpu_custom_call" | custom-call | tf_op jit(solution)/shard_map/finish/pallas_call | solution.py:472

commit v8 on v6

--- a/solution.py
+++ b/solution.py
@@ -43,7 +43,7 @@
     tok_hbm, cot_hbm, gate_hbm, up_hbm, down_hbm,
     tg_out, wg_out, down_out,
     tok_in, cot_in, gate_in, up_in, down_in,
-    wt, wblk, gu, tok, cot, rs_send, rs_recv, hg_send, hg_recv, hg_own, pair,
+    wt, wblk, gu, tok, cot, rs_send, rs_recv, hg_send, hg_recv, pair,
     grads, hid, wg_send, wg_recv, part, ta_send, ta_recv, tb_send, tb_recv, tc_send, tc_recv,
     down_grad, token_grad,
     load_sems, send_sems, recv_sems,
@@ -150,12 +150,12 @@
     cot_core = [send(own, own, at(c_=cs[1]))]
     arrive(tok_first)
     tok_later = [spread(p) for p in range(2)]
+    for q in range(1, NZH):
+        weights.append(send_weights(order[q]))
     cot_far.wait_recv()
     own = cot.at[far // 2, far % 2, c, y]
     cot_y = {k: send(own, own, at(y_=ys[k])) for k in (2, 1, 3)}
     cot_core.append(send(own, own, at(c_=cs[1])))
-    for q in range(1, NZH):
-        weights.append(send_weights(order[q]))
 
     def assemble(q):
         arrive(weights[q])
@@ -182,7 +182,10 @@
         return row
 
     def onward(step, p, row):
-        terms = [partial(ring(4 - step), p), partial(ring(step - 4), p)]
+        there = [ring(4 - step), ring(step - 4)]
+        rows = [gu[:, one[0]].reshape(2 * SUB, HALF) for one in there]
+        both = nt(jnp.concatenate(rows, axis=0), tok[there[0][1], p].reshape(PHASE, HALF))
+        terms = both.reshape(2, 2, SUB, PHASE)
         later = []
         for d in range(2):
             row[d].wait_recv()
@@ -197,24 +200,15 @@
             later.append(send(rs_send.at[p, d, step], rs_recv.at[p, d, step], around[d]))
         return later
 
-    def hidden_part(q, p):
-        rows = down_in[pl.ds(pl.multiple_of(q * SUB, 16), SUB), :]
-        return nt(rows, cot[:, p].reshape(2 * PHASE, HALF))
-
     def hidden_over_x(p):
-        copies = []
-        for k in (2, 1, 3):
-            some = hidden_part(xs[k], p).astype(BF16)
-            for half in range(2):
-                hg_send[p, k - 1, half] = some[:, half * PHASE : (half + 1) * PHASE]
-            copies.append(send(hg_send.at[p, k - 1], hg_recv.at[p, k - 1], at(x_=xs[k])))
-        some = hidden_part(x, p)
+        full = nt(down_in[...], cot[:, p].reshape(2 * PHASE, HALF)).astype(BF16)
         for half in range(2):
-            hg_own[p, half] = some[:, half * PHASE : (half + 1) * PHASE]
-        return copies
+            some = full[:, half * PHASE : (half + 1) * PHASE]
+            hg_send[p, :, half] = some.reshape(NX, SUB, PHASE)
+        return [send(hg_send.at[p, xs[k]], hg_recv.at[p, k - 1], at(x_=xs[k])) for k in (2, 1, 3)]
 
     def hidden_sum(p, half):
-        total = hg_own[p, half]
+        total = hg_send[p, x, half].astype(F32)
         for k in range(NX - 1):
             total = total + hg_recv[p, k, half].astype(F32)
         return total
@@ -440,9 +434,8 @@
         pltpu.VMEM((2, 2, 2, NY, 32, HALF), BF16),
         pltpu.VMEM((2, 2, 4, 2, SUB, PHASE), BF16),
         pltpu.VMEM((2, 2, 4, 2, SUB, PHASE), BF16),
+        pltpu.VMEM((2, NX, 2, SUB, PHASE), BF16),
         pltpu.VMEM((2, NX - 1, 2, SUB, PHASE), BF16),
-        pltpu.VMEM((2, NX - 1, 2, SUB, PHASE), BF16),
-        pltpu.VMEM((2, 2, SUB, PHASE), F32),
         pltpu.VMEM((2, 2, SUB, PHASE), BF16),
         pltpu.VMEM((2, 2, 2, NZH, SUB, PHASE), BF16),
         pltpu.VMEM((2, 2, NX, SUB, PHASE), BF16),

time: 89 us -> 88.9 us (level)
  no operation moved by 1% of the time
where the time goes in v8:
time: 88.9 us; the launch traced here: 88.5 us
  Pallas kernels  87.8 us (99%)
    pallas_call x1, Pallas kernels, shards(): pl.pallas_call(kernel, out_shape=between, in_specs=[hbm] * 5, out_specs=[...  84.8 us
    pallas_call x1, Pallas kernels, shards(): pl.pallas_call(finish, out_shape=outs, in_specs=[hbm] * 3, out_specs=[hbm...  2.98 us

profile of v8, /device:TPU:1, one launch (start us, length us, event | category | flops | bytes accessed | tf_op | source)
XLA Modules:
  0.0 88.5 jit_solution(8214921712338915965)
XLA Ops:
  0.6 84.8 %layer.1 = (f32[32,512]{1,0:T(8,128)}, bf16[4,2,4,112,128]{4,3,2,1,0:T(8,128)(2,1)}, f32[448,512]{1,0:T(8,128)}) custom-call(bf16[32,512]{1,0:T(8,128)(2,1)} %tok_hbm.1, bf16[32,512]{1,0:T(8,128)(2,1)} %cot_hbm.1, bf16[64,3584]{1,0:T(8,128)(2,1)} %gate_hbm.1, bf16[64,3584]{1,0:T(8,128)(2,1)} %up_hbm.1, bf16[448,512]{1,0:T(8,128)(2,1)} %down_hbm.1), custom_call_target="tpu_custom_call" | custom-call | tf_op jit(solution)/shard_map/layer/pallas_call | solution.py:457
  85.5 3.0 %finish.1 = (f32[32,512]{1,0:T(8,128)}, f32[64,3584]{1,0:T(8,128)}, f32[64,3584]{1,0:T(8,128)}, f32[448,512]{1,0:T(8,128)}) custom-call(f32[32,512]{1,0:T(8,128)} %get-tuple-element.7.tg_in, bf16[4,2,4,112,128]{4,3,2,1,0:T(8,128)(2,1)} %get-tuple-element.8.wg_in, f32[448,512]{1,0:T(8,128)} %get-tuple-element.9.down_in), custom_call_target="tpu_custom_call" | custom-call | tf_op jit(solution)/shard_map/finish/pallas_call | solution.py:468
